TPU v7x, 1024 devices: a whole 4x4x32 slice. The times are simulated.
1024 devices in a mesh: vp: 128 (over z, y), op: 8 (over x, core).
Axes of the slice: x: 4, y: 4, z: 32, core: 2. Of those that a mesh axis runs over, the one named last changes fastest.
Arguments:
- amplitudes: float32 [512, 16384], P('op', 'vp'), may hold values from -6 to 6
- integrals: float32 [128, 32, 128, 128], P('vp', None, 'op'), may hold values from -0.09375 to 0.09375
- rest: float32 [512, 16384], P('op', 'vp'), may hold values from -6 to 6
- occ_energy: float32 [512], P('op'), may hold values from -3 to -0.5
- vir_energy: float32 [16384], P('vp'), may hold values from 0.5 to 6
- block_irrep: int32 [128], replicated, may hold values from 0 to 7, as said below
Outputs:
- new_amplitudes: float32 [512, 16384], P('op', 'vp')
Inputs may be any that keep to these rules, and one draw needn't show every extreme that they name: `block_irrep`: no irrep labels more than 32 blocks, and one labels exactly 32; slots k of integrals[position[b]] at or past count[b] are not used.
All inputs are finite; a program needn't handle non-finite values.
Results may differ from a plain program's by a relative error of at most 0.0003.
Values sent between devices are 32-bit elements; how exact they have to be, the bound alone decides.
No kernel may reach another device: no remote copies, remote signals or barrier semaphores. Data moves between devices by JAX's collectives and lax.ppermute only.
A program may use at most 32 MiB of HBM per device.

v0:
```python
import jax
import jax.numpy as jnp
from jax import lax
from jax.sharding import PartitionSpec as P


def per_device(amplitudes, integrals, rest, occ_energy, vir_energy, block_irrep):
    slot_count = integrals.shape[1]
    pair_width = integrals.shape[3]
    count_blocks = block_irrep.shape[0]
    row_count = amplitudes.shape[0]
    piece_width = row_count * pair_width // count_blocks
    positions = jnp.arange(count_blocks, dtype=jnp.int32)
    same = (block_irrep[:, None] == block_irrep[None, :]).astype(jnp.int32)
    earlier = (positions[None, :] < positions[:, None]).astype(jnp.int32)
    rank = jnp.sum(same * earlier, axis=1)
    counts = jnp.sum(same, axis=1)
    lower = jnp.sum((block_irrep[None, :] < block_irrep[:, None]).astype(jnp.int32), axis=1)
    place = lower + rank
    onehot = (place[:, None] == positions[None, :]).astype(jnp.int32)
    order = jnp.sum(onehot * positions[:, None], axis=0)
    here = lax.axis_index("vp")
    block_here = jnp.take(order, here)
    rank_here = jnp.take(rank, block_here)
    count_here = jnp.take(counts, block_here)
    slots = jnp.arange(slot_count, dtype=jnp.int32)
    slot_mask = (slots < count_here).astype(jnp.float32)
    weights = lax.all_gather(integrals, "op", axis=2, tiled=True)[0]
    partner = jnp.take(order, jnp.clip(here - rank_here + slots, 0, count_blocks - 1))
    gathered = lax.all_gather(amplitudes, "vp", axis=1, tiled=True)
    blocks = gathered.reshape(row_count, count_blocks, pair_width)
    picked = jnp.take(blocks, partner, axis=1) * slot_mask[None, :, None]
    ladder = jnp.einsum("qkc,kac->qa", picked, weights, precision=lax.Precision.HIGHEST)
    flat = ladder.reshape(count_blocks, piece_width)
    back = lax.all_to_all(flat, "vp", split_axis=0, concat_axis=0, tiled=True)
    restored = jnp.take(back, place, axis=0)
    ladder = lax.all_to_all(restored, "vp", split_axis=0, concat_axis=0, tiled=True).reshape(
        row_count, pair_width
    )
    return (ladder + rest) / (vir_energy[None, :] - occ_energy[:, None])


def solution(mesh):
    return jax.shard_map(
        per_device,
        mesh=mesh,
        in_specs=(P("op", "vp"), P("vp", None, "op", None), P("op", "vp"), P("op"), P("vp"), P()),
        out_specs=P("op", "vp"),
        check_vma=False,
    )
```

profile of v0, /device:TPU:1, one launch (start us, length us, event | category | flops | bytes accessed | tf_op | source)
XLA Modules:
  0.0 420.3 jit_solution(10356126136167068224)
XLA Ops:
  6.5 0.0 all-gather.3.cloned.1.call-start
  6.5 0.7 all-gather.3.cloned.1.call-update
  7.3 0.0 all-gather.5.cloned.1.call-start
  7.3 0.7 all-gather.5.cloned.1.call-update
  8.0 0.9 convert_reduce_fusion
  9.0 0.1 select_reduce_fusion
  9.1 0.6 dynamic-slice.6
  10.3 0.6 dynamic-slice.7
  10.9 0.6 dynamic-slice.8
  12.8 0.7 gather_fusion
  13.5 254.0 %all-gather.3.cloned.1.call-done = f32[64,16384]{1,0:T(8,128)} async-done(((f32[64,128]{1,0:T(8,128)}), f32[64,16384]{1,0:T(8,128)}) %all-gather.3.cloned.1.call-update) | async-done | bytes 4194320 | tf_op jit(solution)/shard_map/all_gather | solution.py:30
  267.5 4.7 %copy_bitcast_fusion = f32[64,128,128]{2,0,1:T(8,128)} fusion(f32[64,16384]{1,0:T(8,128)} %all-gather.3.cloned.1.call-done), kind=kLoop, calls=%fused_computation.3 | loop fusion | bytes 8388608 | tf_op jit(solution)/shard_map/reshape | solution.py:31
  272.3 0.0 copy-start
  272.3 0.0 copy-start.1
  272.3 0.0 copy-start.2
  272.3 2.8 gather_fusion.1
  275.1 49.1 %all-gather.5.cloned.1.call-done = f32[1,32,128,128]{3,2,1,0:T(8,128)} async-done(((f32[1,32,16,128]{3,2,1,0:T(8,128)}), f32[1,32,128,128]{3,2,1,0:T(8,128)}) %all-gather.5.cloned.1.call-update) | async-done | bytes 2097168 | tf_op jit(solution)/shard_map/all_gather | solution.py:28
  324.2 3.9 fusion.2
  328.1 0.7 all_to_all.12
  328.8 26.9 %all-to-all-start = ((f32[128,1,64]{2,1,0:T(1,128)}), f32[128,1,64]{2,1,0:T(1,128)S(1)}, u32[]{:S(2)}, u32[]{:S(2)}) async-start(f32[128,1,64]{2,1,0:T(1,128)} %bitcast.11), calls=%async_computation | async-start | bytes 131072 | tf_op jit(solution)/shard_map/all_to_all | solution.py:35
  355.7 23.2 %all-to-all-done = f32[128,1,64]{2,1,0:T(1,128)S(1)} async-done(((f32[128,1,64]{2,1,0:T(1,128)}), f32[128,1,64]{2,1,0:T(1,128)S(1)}, u32[]{:S(2)}, u32[]{:S(2)}) %all-to-all-start) | async-done | bytes 32800 | tf_op jit(solution)/shard_map/all_to_all | solution.py:35
  379.0 0.6 gather_fusion.2
  379.6 0.1 bitcast_select_fusion
  379.7 31.7 %all_to_all.18 = f32[128,1,64]{2,1,0:T(1,128)S(1)} all-to-all(f32[128,1,64]{2,1,0:T(1,128)S(1)} %bitcast.38), channel_id=1, replica_groups=mesh['vp'=128,'op'=8] {'vp'}, dimensions={0} | all-to-all | bytes 65536 | tf_op jit(solution)/shard_map/all_to_all | solution.py:37
  411.3 0.5 broadcast.254
  411.9 0.8 reduce.3
  412.7 0.1 reshape.135
  412.7 0.0 copy-done
  412.8 0.0 copy-done.1
  412.8 0.0 copy-done.2
  412.8 0.7 subtract_divide_fusion
  (8 shorter events, 0.1 us)
Async XLA Ops:
  6.5 261.0 %all-gather.3.cloned.1.call-start = ((), (), s32[]{:S(2)}) async-start(), calls=%async_computation.2 | async-start | bytes 4227072 | tf_op jit(solution)/shard_map/all_gather | solution.py:30
  7.3 316.9 %all-gather.5.cloned.1.call-start = ((), (), s32[]{:S(2)}) async-start(), calls=%async_computation.3 | async-start | bytes 2359296 | tf_op jit(solution)/shard_map/all_gather | solution.py:28
  272.3 140.5 %copy-start = (f32[64,128]{1,0:T(8,128)S(1)}, f32[64,128]{1,0:T(8,128)}, u32[]{:S(2)}) copy-start(f32[64,128]{1,0:T(8,128)} %param.8) | copy-start | bytes 98308
  272.3 140.5 %copy-start.1 = (f32[64]{0:T(128)S(1)}, f32[64]{0:T(128)}, u32[]{:S(2)}) copy-start(f32[64]{0:T(128)} %param.9) | copy-start | bytes 772
  272.3 140.5 %copy-start.2 = (f32[128]{0:T(128)S(1)}, f32[128]{0:T(128)}, u32[]{:S(2)}) copy-start(f32[128]{0:T(128)} %param.10) | copy-start | bytes 1540
  328.8 50.2 %all-to-all-start = ((f32[128,1,64]{2,1,0:T(1,128)}), f32[128,1,64]{2,1,0:T(1,128)S(1)}, u32[]{:S(2)}, u32[]{:S(2)}) async-start(f32[128,1,64]{2,1,0:T(1,128)} %bitcast.11), calls=%async_computation | async-start | bytes 131072 | tf_op jit(solution)/shard_map/all_to_all | solution.py:35
Sparse Core Ops, SparseCore 0:
  11.4 256.0 all-gather.2
  270.2 53.9 all-gather.4
where the time goes:
time: 422 us; the launch traced here: 420 us
  waiting for transfers between devices  328 us (78%)
  blocking collectives  31.7 us (8%)
  starting transfers between devices  27 us (6%)
  between operations  15.4 us (4%)
  local copies, waits for them, and re-layouts  12 us (3%)
    all_gather x1, waiting for transfers between devices, per_device(): gathered = lax.all_gather(amplitudes, 'vp', axis=1, tiled=True)  254 us
    all_gather x1, waiting for transfers between devices, per_device(): weights = lax.all_gather(integrals, 'op', axis=2, tiled=True)[0]  49.1 us
    all_to_all x1, blocking collectives, per_device(): lax.all_to_all(restored, 'vp', split_axis=0, concat_axis=0, tiled=True)  31.7 us
    all_to_all x1, starting transfers between devices, per_device(): back = lax.all_to_all(flat, 'vp', split_axis=0, concat_axis=0, tiled=True)  26.9 us
    all_to_all x1, waiting for transfers between devices, per_device(): back = lax.all_to_all(flat, 'vp', split_axis=0, concat_axis=0, tiled=True)  23.2 us
  transfers between devices with their start and end apart: 3, of which 3 were waited for; matrix products, arithmetic and copies ran while one was open for 3% of the time, Pallas kernels for 0%

commit v1 on v0

v1 whole, which is shorter than its diff:
```python
import functools

import jax
import jax.numpy as jnp
from jax import lax
from jax.experimental import pallas as pl
from jax.experimental.pallas import tpu as pltpu
from jax.sharding import Mesh, PartitionSpec as P

HI, LO, Y, X, C = 8, 4, 4, 4, 2
IRREPS = 8
CLASSES = X * C
VP = ("h", "l", "y")
OP = ("x", "c")
PLANE = ("y", "x", "c")
OUT_FIRST, HOME_FIRST = 20, 16
WHOLE = pl.BlockSpec(memory_space=pltpu.VMEM)


def starts_of(irreps):
    name = lax.broadcasted_iota(jnp.int32, (IRREPS, irreps.shape[1]), 0)
    return jnp.sum((irreps < name).astype(jnp.int32), axis=1, keepdims=True)


def places_of(irreps):
    blocks = irreps.shape[1]
    own = jnp.broadcast_to(irreps.astype(jnp.float32), (blocks, blocks))
    other = own.T
    own_id = lax.broadcasted_iota(jnp.int32, (blocks, blocks), 1)
    other_id = lax.broadcasted_iota(jnp.int32, (blocks, blocks), 0)
    before = (other < own) | ((other == own) & (other_id < own_id))
    return jnp.sum(before.astype(jnp.float32), axis=0, keepdims=True).astype(jnp.int32)


def pick_rows(chosen, value):
    hot = chosen.astype(jnp.float32).astype(jnp.bfloat16)
    high, rest = split(value)
    low = (value - high.astype(jnp.float32) - rest.astype(jnp.float32)).astype(jnp.bfloat16)
    total = jnp.dot(hot, low, preferred_element_type=jnp.float32)
    total = total + jnp.dot(hot, rest, preferred_element_type=jnp.float32)
    return total + jnp.dot(hot, high, preferred_element_type=jnp.float32)


def copy_kernel(amplitudes_ref, out_ref):
    for hi in range(HI):
        out_ref[hi] = amplitudes_ref[...]


def roll_kernel(irreps_ref, integrals_ref, keep_ref, give_ref):
    starts = starts_of(irreps_ref[...])
    here = lax.axis_index(VP)
    mine = lax.axis_index(OP)
    first = jnp.max(jnp.where(starts <= here, starts, 0))
    for core, out_ref in enumerate((keep_ref, give_ref)):
        for d in range(X):
            slot = ((mine ^ (d * C + core)) - first) & (CLASSES - 1)
            for turn in range(out_ref.shape[1]):
                out_ref[d, turn] = integrals_ref[turn * CLASSES + slot]


def spread_kernel(irreps_ref, blocks_ref, _, __, out_ref, *, share):
    blocks = irreps_ref.shape[1]
    held = blocks // CLASSES
    row = lax.broadcasted_iota(jnp.int32, (blocks, blocks), 0)
    position = (row % held) * CLASSES + row // held
    sources = pltpu.roll(places_of(irreps_ref[...]), blocks - OUT_FIRST * Y, 1)
    chosen = sources == position
    for r in range(share):
        picked = pick_rows(chosen, blocks_ref[pl.ds(r, blocks, stride=share), :]).reshape(CLASSES, held, -1)
        for column in range(Y):
            out_ref[column, :, pl.ds(r * held, held), :] = picked


def split(value):
    high = value.astype(jnp.bfloat16)
    return high, (value - high.astype(jnp.float32)).astype(jnp.bfloat16)


def dot_nt(a, b):
    return lax.dot_general(a, b, (((1,), (1,)), ((), ())), preferred_element_type=jnp.float32)


def ladder_kernel(irreps_ref, blocks_ref, *refs, sources, held, share):
    weights_refs, out_ref = refs[:-1], refs[-1]
    blocks = irreps_ref.shape[1]
    turns, width = weights_refs[0].shape[1], weights_refs[0].shape[3]
    starts = starts_of(irreps_ref[...])
    mine = lax.axis_index(OP)
    for step, weights_ref in enumerate(weights_refs):
        low = lax.axis_index("l") ^ step
        spot = (lax.axis_index("h") * LO + low) * Y + lax.axis_index("y")
        begun = starts <= spot
        first = jnp.max(jnp.where(begun, starts, 0))
        count = jnp.min(jnp.where(begun, blocks, starts)) - first
        lhs, rhs = [], []
        for turn in range(turns):
            slot = turn * CLASSES + ((mine - first) & (CLASSES - 1))
            m = jnp.minimum((first + slot) // CLASSES, held - 1)
            rows = jnp.concatenate(
                [blocks_ref[pl.ds(r * held + m, sources, stride=share * held), :] for r in range(share)], axis=0
            )
            lhs.append(jnp.where(slot < count, rows, 0.0))
            rhs.append(jnp.concatenate([weights_ref[mine ^ i, turn] for i in range(CLASSES)], axis=0))
        a_high, a_low = split(jnp.concatenate(lhs, axis=1))
        b_high, b_low = split(jnp.concatenate(rhs, axis=1))
        rows = a_high.shape[0]
        both = dot_nt(jnp.concatenate([a_high, a_low], axis=0), b_high)
        total = both[:rows] + both[rows:] + dot_nt(a_high, b_low)
        for r in range(share):
            out_ref[pl.ds(share * step + r, sources, stride=share * LO), :] = total[r * sources : (r + 1) * sources]


def exchange(pieces, first):
    blocks = pieces.shape[0]
    members = [(first * Y + i) % blocks for i in range(blocks)]
    return lax.all_to_all(
        pieces, VP, split_axis=0, concat_axis=0, tiled=True, axis_index_groups=[members]
    )


def per_device(amplitudes, integrals, rest, occ_energy, vir_energy, block_irrep):
    rows, width = amplitudes.shape
    slots = integrals.shape[1]
    part = integrals.shape[2]
    blocks = block_irrep.shape[0]
    group = blocks // HI
    turns = slots // CLASSES
    held = blocks // CLASSES
    sources = Y * CLASSES
    share = rows // (LO * Y)
    irreps = block_irrep.reshape(1, blocks)

    spread = pl.pallas_call(
        copy_kernel,
        out_shape=jax.ShapeDtypeStruct((HI, rows, width), jnp.float32),
        in_specs=[WHOLE],
        out_specs=WHOLE,
        name="copy_rows",
    )(amplitudes)
    spread = exchange(spread.reshape(blocks, share, width), OUT_FIRST)

    keep, give = pl.pallas_call(
        roll_kernel,
        out_shape=[jax.ShapeDtypeStruct((X, turns, part, width), jnp.float32)] * C,
        in_specs=[WHOLE] * 2,
        out_specs=[WHOLE] * C,
        compiler_params=pltpu.CompilerParams(vmem_limit_bytes=24 * 1024 * 1024),
        name="roll_slots",
    )(irreps, integrals[0])
    cores = jnp.stack([keep, lax.ppermute(give, "c", [(i, i ^ 1) for i in range(C)])], axis=1)
    own = jnp.concatenate(
        [cores[0]] + [lax.ppermute(cores[d], "x", [(i, i ^ d) for i in range(X)]) for d in range(1, X)], axis=0
    )
    far = lax.ppermute(own, "l", [(i, i ^ 2) for i in range(LO)])
    near = lax.ppermute(own, "l", [(i, i ^ 1) for i in range(LO)])
    weights = [own, near, far, lax.ppermute(far, "l", [(i, i ^ 1) for i in range(LO)])]

    by_class = pl.pallas_call(
        functools.partial(spread_kernel, share=share),
        out_shape=jax.ShapeDtypeStruct((Y, CLASSES, share * held, width), jnp.float32),
        in_specs=[WHOLE, WHOLE] + [pl.BlockSpec(memory_space=pl.ANY)] * 2,
        out_specs=WHOLE,
        compiler_params=pltpu.CompilerParams(vmem_limit_bytes=24 * 1024 * 1024),
        name="spread_classes",
    )(irreps, spread.reshape(share * blocks, width), far, near)
    by_class = lax.all_to_all(
        by_class.reshape(sources, share * held, width), PLANE, split_axis=0, concat_axis=0, tiled=True
    )

    partial = pl.pallas_call(
        functools.partial(ladder_kernel, sources=sources, held=held, share=share),
        out_shape=jax.ShapeDtypeStruct((sources * share * LO, width), jnp.float32),
        in_specs=[WHOLE] * (2 + LO),
        out_specs=WHOLE,
        compiler_params=pltpu.CompilerParams(vmem_limit_bytes=24 * 1024 * 1024),
        name="ladder_terms",
    )(irreps, by_class.reshape(sources * share * held, width), *weights)

    partial = lax.all_to_all(
        partial.reshape(sources, share * LO, width), PLANE, split_axis=0, concat_axis=0, tiled=True
    )
    ladder = jnp.sum(partial.reshape(Y, CLASSES, share * LO, width), axis=1).reshape(group, share, width)

    ids = jnp.arange(blocks, dtype=jnp.int32)
    same = block_irrep[:, None] == block_irrep[None, :]
    before = (block_irrep[None, :] < block_irrep[:, None]) | (same & (ids[None, :] < ids[:, None]))
    place = jnp.sum(before.astype(jnp.int32), axis=1)
    local = jnp.clip(place - lax.axis_index("h") * group, 0, group - 1)
    at = (local % Y) * LO + ((local // Y) ^ lax.axis_index("l"))
    at = jnp.roll(at, -HOME_FIRST * Y)
    home = exchange(ladder.at[at].get(mode="promise_in_bounds"), HOME_FIRST)
    place_here = jnp.sum(jnp.where(ids == lax.axis_index(VP), place, 0))
    home = lax.dynamic_index_in_dim(home.reshape(HI, rows, width), (place_here // group - HOME_FIRST // LO) % HI, 0, False)
    return (home + rest) / (vir_energy[None, :] - occ_energy[:, None])


def solution(mesh):
    split_mesh = Mesh(mesh.devices.reshape(HI, LO, Y, X, C), ("h", "l", "y", "x", "c"))
    return jax.shard_map(
        per_device,
        mesh=split_mesh,
        in_specs=(P(OP, VP), P(VP, None, OP, None), P(OP, VP), P(OP), P(VP), P()),
        out_specs=P(OP, VP),
        check_vma=False,
    )
```

time: 422 us -> 167 us (0.40)
  waiting for transfers between devices: 328 us -> 62.7 us
  starting transfers between devices: 27 us -> 91.7 us
  blocking collectives: 31.7 us -> 0 us
  between operations: 15.4 us -> 2.81 us
  local copies, waits for them, and re-layouts: 12 us -> 2.17 us
  Pallas kernels: 0 us -> 5.37 us
    all_gather x2 -> x0, waiting for transfers between devices: 303 us -> none  [the longest x1 254 us: per_device(): gathered = lax.all_gather(amplitudes, 'vp', axis=1, tiled=True)]
    all_to_all x1 -> x4, starting transfers between devices: 26.9 us -> 70.5 us  [the longest x2 59.1 us: exchange(): lax.all_to_all(pieces, VP, split_axis=0, concat_axis=0, tiled=True, axis_...]
    all_to_all x1 -> x0, blocking collectives: 31.7 us -> none  [per_device(): lax.all_to_all(restored, 'vp', split_axis=0, concat_axis=0, tiled=True)]
    ppermute x0 -> x7, waiting for transfers between devices: none -> 24.4 us  [the longest x1 13.5 us: per_device(): far = lax.ppermute(own, 'l', [(i, i ^ 2) for i in range(LO)])]
    ppermute x0 -> x7, starting transfers between devices: none -> 21.2 us  [the longest x3 8.98 us: per_device(): lax.ppermute(cores[d], 'x', [(i, i ^ d) for i in range(X)])]
    all_to_all x1 -> x4, waiting for transfers between devices: 23.2 us -> 38.3 us  [the longest x2 21.8 us: exchange(): lax.all_to_all(pieces, VP, split_axis=0, concat_axis=0, tiled=True, axis_...]
    pallas_call x0 -> x4, Pallas kernels: none -> 5.37 us  [the longest x1 2.32 us: per_device(): pl.pallas_call(functools.partial(ladder_kernel, sources=sources, held=hel...]
    reshape x2 -> x0, local copies, waits for them, and re-layouts: 4.81 us -> none  [the longest x1 4.74 us: per_device(): blocks = gathered.reshape(row_count, count_blocks, pair_width)]
  transfers between devices with their start and end apart: 3 -> 11, of which waited for: 3 -> 8; matrix products, arithmetic and copies ran while one was open for 3% -> 1% of each run, Pallas kernels for 0% -> 0%
where the time goes in v1:
time: 167 us; the launch traced here: 166 us
  starting transfers between devices  91.7 us (55%)
  waiting for transfers between devices  62.7 us (38%)
  Pallas kernels  5.37 us (3%)
  between operations  2.81 us (2%)
  local copies, waits for them, and re-layouts  2.17 us (1%)
    all_to_all x2, starting transfers between devices, exchange(): lax.all_to_all(pieces, VP, split_axis=0, concat_axis=0, tiled=True, axis_...  59.1 us
    all_to_all x2, waiting for transfers between devices, exchange(): lax.all_to_all(pieces, VP, split_axis=0, concat_axis=0, tiled=True, axis_...  21.8 us
    ppermute x1, waiting for transfers between devices, per_device(): far = lax.ppermute(own, 'l', [(i, i ^ 2) for i in range(LO)])  13.5 us
    ppermute x3, starting transfers between devices, per_device(): lax.ppermute(cores[d], 'x', [(i, i ^ d) for i in range(X)])  8.98 us
    all_to_all x1, waiting for transfers between devices, per_device(): lax.all_to_all(partial.reshape(sources, share * LO, width), PLANE, split_...  8.85 us
    all_to_all x1, waiting for transfers between devices, per_device(): lax.all_to_all(by_class.reshape(sources, share * held, width), PLANE, spl...  7.61 us
    all_to_all x1, starting transfers between devices, per_device(): lax.all_to_all(by_class.reshape(sources, share * held, width), PLANE, spl...  7.53 us
    ppermute x1, waiting for transfers between devices, per_device(): lax.ppermute(far, 'l', [(i, i ^ 1) for i in range(LO)])  6.82 us
  transfers between devices with their start and end apart: 11, of which 8 were waited for; matrix products, arithmetic and copies ran while one was open for 1% of the time, Pallas kernels for 0%

profile of v1, /device:TPU:1, one launch (start us, length us, event | category | flops | bytes accessed | tf_op | source)
XLA Modules:
  0.0 166.4 jit_solution(12710429026370911884)
XLA Ops:
  0.0 1.5 copy_rows.1
  1.5 0.0 copy-start
  1.5 35.5 %all-to-all-start = ((f32[128,4,128]{2,1,0:T(4,128)}), f32[128,4,128]{2,1,0:T(4,128)S(1)}, u32[]{:S(2)}, u32[]{:S(2)}) async-start(f32[128,4,128]{2,1,0:T(4,128)} %bitcast.39), calls=%async_computation | async-start | bytes 524288 | tf_op jit(solution)/shard_map/all_to_all | solution.py:116
  37.0 0.0 copy-start.1
  37.0 0.0 copy-done
  37.0 0.6 copy-done.1
  37.6 0.1 roll_slots.1
  37.8 3.1 %collective-permute-start = (f32[4,4,16,128]{3,2,1,0:T(8,128)S(1)}, f32[4,4,16,128]{3,2,1,0:T(8,128)S(1)}, u32[]{:S(2)}, u32[]{:S(2)}) collective-permute-start(f32[4,4,16,128]{3,2,1,0:T(8,128)S(1)} %get-tuple-element.8), channel_id=1, source_target_pairs={{0,1},{1,0},{2,3},{3,2},{4,5},{5,4},{6,7},{7,6},{8,9},{9,8},{10,11... | collective-permute-start | bytes 393224 | tf_op jit(solution)/shard_map/ppermute | solution.py:150
  40.9 1.0 collective-permute-done
  41.9 4.4 %collective-permute-start.3 = (f32[2,4,16,128]{3,2,1,0:T(8,128)S(1)}, f32[2,4,16,128]{3,2,1,0:T(8,128)S(1)}, u32[]{:S(2)}, u32[]{:S(2)}) collective-permute-start(f32[2,4,16,128]{3,2,1,0:T(8,128)S(1)} %get-tuple-element.11), channel_id=1, source_target_pairs={{0,6},{2,4},{4,2},{6,0},{1,7},{3,5},{5,3},{7,1},{8,14},{10,12},{12... | collective-permute-start | bytes 196616 | tf_op jit(solution)/shard_map/ppermute | solution.py:152
  46.3 2.4 %collective-permute-start.2 = (f32[2,4,16,128]{3,2,1,0:T(8,128)S(1)}, f32[2,4,16,128]{3,2,1,0:T(8,128)S(1)}, u32[]{:S(2)}, u32[]{:S(2)}) collective-permute-start(f32[2,4,16,128]{3,2,1,0:T(8,128)S(1)} %get-tuple-element.12), channel_id=1, source_target_pairs={{0,4},{2,6},{4,0},{6,2},{1,5},{3,7},{5,1},{7,3},{8,12},{10,14},{12... | collective-permute-start | bytes 196616 | tf_op jit(solution)/shard_map/ppermute | solution.py:152
  48.8 2.2 %collective-permute-start.1 = (f32[2,4,16,128]{3,2,1,0:T(8,128)S(1)}, f32[2,4,16,128]{3,2,1,0:T(8,128)S(1)}, u32[]{:S(2)}, u32[]{:S(2)}) collective-permute-start(f32[2,4,16,128]{3,2,1,0:T(8,128)S(1)} %get-tuple-element.10), channel_id=1, source_target_pairs={{0,2},{2,0},{4,6},{6,4},{1,3},{3,1},{5,7},{7,5},{8,10},{10,8},{12,... | collective-permute-start | bytes 196616 | tf_op jit(solution)/shard_map/ppermute | solution.py:152
  50.9 0.0 collective-permute-done.3
  50.9 2.2 %collective-permute-done.2 = f32[2,4,16,128]{3,2,1,0:T(8,128)S(1)} collective-permute-done((f32[2,4,16,128]{3,2,1,0:T(8,128)S(1)}, f32[2,4,16,128]{3,2,1,0:T(8,128)S(1)}, u32[]{:S(2)}, u32[]{:S(2)}) %collective-permute-start.2) | collective-permute-done | bytes 65568 | tf_op jit(solution)/shard_map/ppermute | solution.py:152
  53.1 0.9 collective-permute-done.1
  54.1 4.0 %collective-permute-start.4 = (f32[8,4,16,128]{3,2,1,0:T(8,128)S(1)}, f32[8,4,16,128]{3,2,1,0:T(8,128)S(1)}, u32[]{:S(2)}, u32[]{:S(2)}) collective-permute-start(f32[8,4,16,128]{3,2,1,0:T(8,128)S(1)} %pad_maximum_fusion.refs_0_), channel_id=1, source_target_pairs={{0,64},{32,96},{64,0},{96,32},{1,65},{33,97},{65,1},{97,33},{2,66}... | collective-permute-start | bytes 786440 | tf_op jit(solution)/shard_map/ppermute | solution.py:154
  58.1 3.1 %collective-permute-start.5 = (f32[8,4,16,128]{3,2,1,0:T(8,128)S(1)}, f32[8,4,16,128]{3,2,1,0:T(8,128)S(1)}, u32[]{:S(2)}, u32[]{:S(2)}) collective-permute-start(f32[8,4,16,128]{3,2,1,0:T(8,128)S(1)} %pad_maximum_fusion.refs_0_), channel_id=1, source_target_pairs={{0,32},{32,0},{64,96},{96,64},{1,33},{33,1},{65,97},{97,65},{2,34}... | collective-permute-start | bytes 786440 | tf_op jit(solution)/shard_map/ppermute | solution.py:155
  61.3 13.5 %collective-permute-done.4._.refs_2_ = f32[8,4,16,128]{3,2,1,0:T(8,128)S(1)} collective-permute-done((f32[8,4,16,128]{3,2,1,0:T(8,128)S(1)}, f32[8,4,16,128]{3,2,1,0:T(8,128)S(1)}, u32[]{:S(2)}, u32[]{:S(2)}) %collective-permute-start.4) | collective-permute-done | bytes 262176 | tf_op jit(solution)/shard_map/ppermute | solution.py:154
  74.8 0.0 collective-permute-done.5.__.refs_1_
  74.8 0.0 all-to-all-done
  74.8 1.4 spread_classes.1
  76.2 7.5 %all-to-all-start.1 = ((f32[32,64,128]{2,1,0:T(8,128)}), f32[32,64,128]{2,1,0:T(8,128)S(1)}, u32[]{:S(2)}, u32[]{:S(2)}) async-start(f32[32,64,128]{2,1,0:T(8,128)} %bitcast.10), calls=%async_computation.1 | async-start | bytes 2097152 | tf_op jit(solution)/shard_map/all_to_all | solution.py:166
  83.8 1.9 %collective-permute-start.6 = (f32[8,4,16,128]{3,2,1,0:T(8,128)S(1)}, f32[8,4,16,128]{3,2,1,0:T(8,128)S(1)}, u32[]{:S(2)}, u32[]{:S(2)}) collective-permute-start(f32[8,4,16,128]{3,2,1,0:T(8,128)S(1)} %collective-permute-done.4._.refs_2_), channel_id=1, source_target_pairs={{0,32},{32,0},{64,96},{96,64},{1,33},{33,1},{65,97},{97,65},{2,34}... | collective-permute-start | bytes 786440 | tf_op jit(solution)/shard_map/ppermute | solution.py:156
  85.7 0.2 convert_reduce_fusion
  85.9 0.6 fusion.12
  86.5 6.8 %collective-permute-done.6.refs_3_ = f32[8,4,16,128]{3,2,1,0:T(8,128)S(1)} collective-permute-done((f32[8,4,16,128]{3,2,1,0:T(8,128)S(1)}, f32[8,4,16,128]{3,2,1,0:T(8,128)S(1)}, u32[]{:S(2)}, u32[]{:S(2)}) %collective-permute-start.6) | collective-permute-done | bytes 262176 | tf_op jit(solution)/shard_map/ppermute | solution.py:156
  93.3 7.6 %all-to-all-done.1 = f32[32,64,128]{2,1,0:T(8,128)S(1)} async-done(((f32[32,64,128]{2,1,0:T(8,128)}), f32[32,64,128]{2,1,0:T(8,128)S(1)}, u32[]{:S(2)}, u32[]{:S(2)}) %all-to-all-start.1) | async-done | bytes 1048608 | tf_op jit(solution)/shard_map/all_to_all | solution.py:166
  100.9 2.3 %ladder_terms.1 = f32[512,128]{1,0:T(8,128)} custom-call(s32[1,128]{1,0:T(1,128)S(1)} %bitcast.37, f32[2048,128]{1,0:T(8,128)S(1)} %bitcast.31, f32[8,4,16,128]{3,2,1,0:T(8,128)S(1)} %pad_maximum_fusion.refs_0_, f32[8,4,16,128]{3,2,1,0:T(8,128)S(1)} %collective-permute-done.5.__.refs_1_, f32[8,4,16,128]{3,2,1,0:T(8,128)S(1)} %collective-permute-done.4._.refs_2_, ...), custom_call_target="tpu_custom_call" | custom-call | tf_op jit(solution)/shard_map/ladder_terms/pallas_call | solution.py:170
  103.2 3.9 %all-to-all-start.2 = ((f32[32,16,128]{2,1,0:T(8,128)}), f32[32,16,128]{2,1,0:T(8,128)S(1)}, u32[]{:S(2)}, u32[]{:S(2)}) async-start(f32[32,16,128]{2,1,0:T(8,128)} %bitcast.12), calls=%async_computation.2 | async-start | bytes 524288 | tf_op jit(solution)/shard_map/all_to_all | solution.py:179
  107.2 0.1 slice_bitcast_fusion.1
  107.2 0.1 fusion.13
  107.3 8.9 %all-to-all-done.2 = f32[32,16,128]{2,1,0:T(8,128)S(1)} async-done(((f32[32,16,128]{2,1,0:T(8,128)}), f32[32,16,128]{2,1,0:T(8,128)S(1)}, u32[]{:S(2)}, u32[]{:S(2)}) %all-to-all-start.2) | async-done | bytes 262176 | tf_op jit(solution)/shard_map/all_to_all | solution.py:179
  116.2 1.4 gather_fusion
  117.6 23.6 %all-to-all-start.3 = ((f32[128,4,128]{2,1,0:T(4,128)}), f32[128,4,128]{2,1,0:T(4,128)S(1)}, u32[]{:S(2)}, u32[]{:S(2)}) async-start(f32[128,4,128]{2,1,0:T(4,128)} %gather_fusion), calls=%async_computation.3 | async-start | bytes 524288 | tf_op jit(solution)/shard_map/all_to_all | solution.py:116
  141.2 0.0 copy-start.2
  143.8 0.0 copy-start.3
  143.9 0.0 copy-start.4
  143.9 21.8 %all-to-all-done.3 = f32[128,4,128]{2,1,0:T(4,128)S(1)} async-done(((f32[128,4,128]{2,1,0:T(4,128)}), f32[128,4,128]{2,1,0:T(4,128)S(1)}, u32[]{:S(2)}, u32[]{:S(2)}) %all-to-all-start.3) | async-done | bytes 262176 | tf_op jit(solution)/shard_map/all_to_all | solution.py:116
  165.7 0.0 copy-done.2
  165.7 0.0 copy-done.3
  165.7 0.0 copy-done.4
  165.7 0.7 fusion.9
  (4 shorter events, 0.1 us)
Async XLA Ops:
  1.5 35.5 %copy-start = (f32[1,32,16,128]{3,2,1,0:T(8,128)S(1)}, f32[1,32,16,128]{3,2,1,0:T(8,128)}, u32[]{:S(2)}) copy-start(f32[1,32,16,128]{3,2,1,0:T(8,128)} %param.7) | copy-start | bytes 786436
  1.5 73.3 %all-to-all-start = ((f32[128,4,128]{2,1,0:T(4,128)}), f32[128,4,128]{2,1,0:T(4,128)S(1)}, u32[]{:S(2)}, u32[]{:S(2)}) async-start(f32[128,4,128]{2,1,0:T(4,128)} %bitcast.39), calls=%async_computation | async-start | bytes 524288 | tf_op jit(solution)/shard_map/all_to_all | solution.py:116
  37.0 0.7 copy-start.1
  37.8 4.1 %collective-permute-start = (f32[4,4,16,128]{3,2,1,0:T(8,128)S(1)}, f32[4,4,16,128]{3,2,1,0:T(8,128)S(1)}, u32[]{:S(2)}, u32[]{:S(2)}) collective-permute-start(f32[4,4,16,128]{3,2,1,0:T(8,128)S(1)} %get-tuple-element.8), channel_id=1, source_target_pairs={{0,1},{1,0},{2,3},{3,2},{4,5},{5,4},{6,7},{7,6},{8,9},{9,8},{10,11... | collective-permute-start | bytes 393224 | tf_op jit(solution)/shard_map/ppermute | solution.py:150
  41.9 9.0 %collective-permute-start.3 = (f32[2,4,16,128]{3,2,1,0:T(8,128)S(1)}, f32[2,4,16,128]{3,2,1,0:T(8,128)S(1)}, u32[]{:S(2)}, u32[]{:S(2)}) collective-permute-start(f32[2,4,16,128]{3,2,1,0:T(8,128)S(1)} %get-tuple-element.11), channel_id=1, source_target_pairs={{0,6},{2,4},{4,2},{6,0},{1,7},{3,5},{5,3},{7,1},{8,14},{10,12},{12... | collective-permute-start | bytes 196616 | tf_op jit(solution)/shard_map/ppermute | solution.py:152
  46.3 6.8 %collective-permute-start.2 = (f32[2,4,16,128]{3,2,1,0:T(8,128)S(1)}, f32[2,4,16,128]{3,2,1,0:T(8,128)S(1)}, u32[]{:S(2)}, u32[]{:S(2)}) collective-permute-start(f32[2,4,16,128]{3,2,1,0:T(8,128)S(1)} %get-tuple-element.12), channel_id=1, source_target_pairs={{0,4},{2,6},{4,0},{6,2},{1,5},{3,7},{5,1},{7,3},{8,12},{10,14},{12... | collective-permute-start | bytes 196616 | tf_op jit(solution)/shard_map/ppermute | solution.py:152
  48.8 5.3 %collective-permute-start.1 = (f32[2,4,16,128]{3,2,1,0:T(8,128)S(1)}, f32[2,4,16,128]{3,2,1,0:T(8,128)S(1)}, u32[]{:S(2)}, u32[]{:S(2)}) collective-permute-start(f32[2,4,16,128]{3,2,1,0:T(8,128)S(1)} %get-tuple-element.10), channel_id=1, source_target_pairs={{0,2},{2,0},{4,6},{6,4},{1,3},{3,1},{5,7},{7,5},{8,10},{10,8},{12,... | collective-permute-start | bytes 196616 | tf_op jit(solution)/shard_map/ppermute | solution.py:152
  54.1 20.7 %collective-permute-start.4 = (f32[8,4,16,128]{3,2,1,0:T(8,128)S(1)}, f32[8,4,16,128]{3,2,1,0:T(8,128)S(1)}, u32[]{:S(2)}, u32[]{:S(2)}) collective-permute-start(f32[8,4,16,128]{3,2,1,0:T(8,128)S(1)} %pad_maximum_fusion.refs_0_), channel_id=1, source_target_pairs={{0,64},{32,96},{64,0},{96,32},{1,65},{33,97},{65,1},{97,33},{2,66}... | collective-permute-start | bytes 786440 | tf_op jit(solution)/shard_map/ppermute | solution.py:154
  58.1 16.6 %collective-permute-start.5 = (f32[8,4,16,128]{3,2,1,0:T(8,128)S(1)}, f32[8,4,16,128]{3,2,1,0:T(8,128)S(1)}, u32[]{:S(2)}, u32[]{:S(2)}) collective-permute-start(f32[8,4,16,128]{3,2,1,0:T(8,128)S(1)} %pad_maximum_fusion.refs_0_), channel_id=1, source_target_pairs={{0,32},{32,0},{64,96},{96,64},{1,33},{33,1},{65,97},{97,65},{2,34}... | collective-permute-start | bytes 786440 | tf_op jit(solution)/shard_map/ppermute | solution.py:155
  76.2 24.7 %all-to-all-start.1 = ((f32[32,64,128]{2,1,0:T(8,128)}), f32[32,64,128]{2,1,0:T(8,128)S(1)}, u32[]{:S(2)}, u32[]{:S(2)}) async-start(f32[32,64,128]{2,1,0:T(8,128)} %bitcast.10), calls=%async_computation.1 | async-start | bytes 2097152 | tf_op jit(solution)/shard_map/all_to_all | solution.py:166
  83.8 9.6 %collective-permute-start.6 = (f32[8,4,16,128]{3,2,1,0:T(8,128)S(1)}, f32[8,4,16,128]{3,2,1,0:T(8,128)S(1)}, u32[]{:S(2)}, u32[]{:S(2)}) collective-permute-start(f32[8,4,16,128]{3,2,1,0:T(8,128)S(1)} %collective-permute-done.4._.refs_2_), channel_id=1, source_target_pairs={{0,32},{32,0},{64,96},{96,64},{1,33},{33,1},{65,97},{97,65},{2,34}... | collective-permute-start | bytes 786440 | tf_op jit(solution)/shard_map/ppermute | solution.py:156
  103.2 12.9 %all-to-all-start.2 = ((f32[32,16,128]{2,1,0:T(8,128)}), f32[32,16,128]{2,1,0:T(8,128)S(1)}, u32[]{:S(2)}, u32[]{:S(2)}) async-start(f32[32,16,128]{2,1,0:T(8,128)} %bitcast.12), calls=%async_computation.2 | async-start | bytes 524288 | tf_op jit(solution)/shard_map/all_to_all | solution.py:179
  117.6 48.0 %all-to-all-start.3 = ((f32[128,4,128]{2,1,0:T(4,128)}), f32[128,4,128]{2,1,0:T(4,128)S(1)}, u32[]{:S(2)}, u32[]{:S(2)}) async-start(f32[128,4,128]{2,1,0:T(4,128)} %gather_fusion), calls=%async_computation.3 | async-start | bytes 524288 | tf_op jit(solution)/shard_map/all_to_all | solution.py:116
  141.2 24.5 %copy-start.2 = (f32[64,128]{1,0:T(8,128)S(1)}, f32[64,128]{1,0:T(8,128)}, u32[]{:S(2)}) copy-start(f32[64,128]{1,0:T(8,128)} %param.8) | copy-start | bytes 98308
  143.8 21.8 %copy-start.3 = (f32[64]{0:T(128)S(1)}, f32[64]{0:T(128)}, u32[]{:S(2)}) copy-start(f32[64]{0:T(128)} %param.9) | copy-start | bytes 772
  143.9 21.8 %copy-start.4 = (f32[128]{0:T(128)S(1)}, f32[128]{0:T(128)}, u32[]{:S(2)}) copy-start(f32[128]{0:T(128)} %param.10) | copy-start | bytes 1540

commit v2 on v1

--- a/solution.py
+++ b/solution.py
@@ -13,7 +13,7 @@
 VP = ("h", "l", "y")
 OP = ("x", "c")
 PLANE = ("y", "x", "c")
-OUT_FIRST, HOME_FIRST = 20, 16
+OUT_FIRST, HOME_FIRST = 24, 16
 WHOLE = pl.BlockSpec(memory_space=pltpu.VMEM)
 
 

time: 167 us -> 165 us (0.988)
    all_to_all x2, starting transfers between devices: 59.1 us -> 56.9 us  [exchange(): lax.all_to_all(pieces, VP, split_axis=0, concat_axis=0, tiled=True, axis_...]
where the time goes in v2:
time: 165 us
  starting transfers between devices  90.4 us (55%)
  waiting for transfers between devices  62.1 us (38%)
  Pallas kernels  5.37 us (3%)
  between operations  2.81 us (2%)
  local copies, waits for them, and re-layouts  2.17 us (1%)
    all_to_all x2, starting transfers between devices, exchange(): lax.all_to_all(pieces, VP, split_axis=0, concat_axis=0, tiled=True, axis_...  56.9 us
    all_to_all x2, waiting for transfers between devices, exchange(): lax.all_to_all(pieces, VP, split_axis=0, concat_axis=0, tiled=True, axis_...  21.8 us
    ppermute x1, waiting for transfers between devices, per_device(): far = lax.ppermute(own, 'l', [(i, i ^ 2) for i in range(LO)])  13 us
    ppermute x3, starting transfers between devices, per_device(): lax.ppermute(cores[d], 'x', [(i, i ^ d) for i in range(X)])  8.98 us
    all_to_all x1, waiting for transfers between devices, per_device(): lax.all_to_all(partial.reshape(sources, share * LO, width), PLANE, split_...  8.85 us
    all_to_all x1, starting transfers between devices, per_device(): lax.all_to_all(by_class.reshape(sources, share * held, width), PLANE, spl...  8.35 us
    all_to_all x1, waiting for transfers between devices, per_device(): lax.all_to_all(by_class.reshape(sources, share * held, width), PLANE, spl...  7.61 us
    ppermute x1, waiting for transfers between devices, per_device(): lax.ppermute(far, 'l', [(i, i ^ 1) for i in range(LO)])  6.82 us
  transfers between devices with their start and end apart: 11, of which 8 were waited for; matrix products, arithmetic and copies ran while one was open for 1% of the time, Pallas kernels for 0%

profile of v2, /device:TPU:1, one launch (start us, length us, event | category | flops | bytes accessed | tf_op | source)
XLA Modules:
  0.0 164.5 jit_solution(8996350060182328325)
XLA Ops:
  0.0 1.5 copy_rows.1
  1.5 0.0 copy-start
  1.5 33.4 %all-to-all-start = ((f32[128,4,128]{2,1,0:T(4,128)}), f32[128,4,128]{2,1,0:T(4,128)S(1)}, u32[]{:S(2)}, u32[]{:S(2)}) async-start(f32[128,4,128]{2,1,0:T(4,128)} %bitcast.39), calls=%async_computation | async-start | bytes 524288 | tf_op jit(solution)/shard_map/all_to_all | solution.py:116
  34.9 0.0 copy-start.1
  34.9 0.0 copy-done
  34.9 0.6 copy-done.1
  35.5 0.1 roll_slots.1
  35.7 3.1 %collective-permute-start = (f32[4,4,16,128]{3,2,1,0:T(8,128)S(1)}, f32[4,4,16,128]{3,2,1,0:T(8,128)S(1)}, u32[]{:S(2)}, u32[]{:S(2)}) collective-permute-start(f32[4,4,16,128]{3,2,1,0:T(8,128)S(1)} %get-tuple-element.8), channel_id=1, source_target_pairs={{0,1},{1,0},{2,3},{3,2},{4,5},{5,4},{6,7},{7,6},{8,9},{9,8},{10,11... | collective-permute-start | bytes 393224 | tf_op jit(solution)/shard_map/ppermute | solution.py:150
  38.8 1.0 collective-permute-done
  39.8 4.4 %collective-permute-start.3 = (f32[2,4,16,128]{3,2,1,0:T(8,128)S(1)}, f32[2,4,16,128]{3,2,1,0:T(8,128)S(1)}, u32[]{:S(2)}, u32[]{:S(2)}) collective-permute-start(f32[2,4,16,128]{3,2,1,0:T(8,128)S(1)} %get-tuple-element.11), channel_id=1, source_target_pairs={{0,6},{2,4},{4,2},{6,0},{1,7},{3,5},{5,3},{7,1},{8,14},{10,12},{12... | collective-permute-start | bytes 196616 | tf_op jit(solution)/shard_map/ppermute | solution.py:152
  44.2 2.4 %collective-permute-start.2 = (f32[2,4,16,128]{3,2,1,0:T(8,128)S(1)}, f32[2,4,16,128]{3,2,1,0:T(8,128)S(1)}, u32[]{:S(2)}, u32[]{:S(2)}) collective-permute-start(f32[2,4,16,128]{3,2,1,0:T(8,128)S(1)} %get-tuple-element.12), channel_id=1, source_target_pairs={{0,4},{2,6},{4,0},{6,2},{1,5},{3,7},{5,1},{7,3},{8,12},{10,14},{12... | collective-permute-start | bytes 196616 | tf_op jit(solution)/shard_map/ppermute | solution.py:152
  46.6 2.2 %collective-permute-start.1 = (f32[2,4,16,128]{3,2,1,0:T(8,128)S(1)}, f32[2,4,16,128]{3,2,1,0:T(8,128)S(1)}, u32[]{:S(2)}, u32[]{:S(2)}) collective-permute-start(f32[2,4,16,128]{3,2,1,0:T(8,128)S(1)} %get-tuple-element.10), channel_id=1, source_target_pairs={{0,2},{2,0},{4,6},{6,4},{1,3},{3,1},{5,7},{7,5},{8,10},{10,8},{12,... | collective-permute-start | bytes 196616 | tf_op jit(solution)/shard_map/ppermute | solution.py:152
  48.8 0.0 collective-permute-done.3
  48.8 2.2 %collective-permute-done.2 = f32[2,4,16,128]{3,2,1,0:T(8,128)S(1)} collective-permute-done((f32[2,4,16,128]{3,2,1,0:T(8,128)S(1)}, f32[2,4,16,128]{3,2,1,0:T(8,128)S(1)}, u32[]{:S(2)}, u32[]{:S(2)}) %collective-permute-start.2) | collective-permute-done | bytes 65568 | tf_op jit(solution)/shard_map/ppermute | solution.py:152
  51.0 0.9 collective-permute-done.1
  52.0 4.0 %collective-permute-start.4 = (f32[8,4,16,128]{3,2,1,0:T(8,128)S(1)}, f32[8,4,16,128]{3,2,1,0:T(8,128)S(1)}, u32[]{:S(2)}, u32[]{:S(2)}) collective-permute-start(f32[8,4,16,128]{3,2,1,0:T(8,128)S(1)} %pad_maximum_fusion.refs_0_), channel_id=1, source_target_pairs={{0,64},{32,96},{64,0},{96,32},{1,65},{33,97},{65,1},{97,33},{2,66}... | collective-permute-start | bytes 786440 | tf_op jit(solution)/shard_map/ppermute | solution.py:154
  56.0 3.1 %collective-permute-start.5 = (f32[8,4,16,128]{3,2,1,0:T(8,128)S(1)}, f32[8,4,16,128]{3,2,1,0:T(8,128)S(1)}, u32[]{:S(2)}, u32[]{:S(2)}) collective-permute-start(f32[8,4,16,128]{3,2,1,0:T(8,128)S(1)} %pad_maximum_fusion.refs_0_), channel_id=1, source_target_pairs={{0,32},{32,0},{64,96},{96,64},{1,33},{33,1},{65,97},{97,65},{2,34}... | collective-permute-start | bytes 786440 | tf_op jit(solution)/shard_map/ppermute | solution.py:155
  59.1 13.0 %collective-permute-done.4._.refs_2_ = f32[8,4,16,128]{3,2,1,0:T(8,128)S(1)} collective-permute-done((f32[8,4,16,128]{3,2,1,0:T(8,128)S(1)}, f32[8,4,16,128]{3,2,1,0:T(8,128)S(1)}, u32[]{:S(2)}, u32[]{:S(2)}) %collective-permute-start.4) | collective-permute-done | bytes 262176 | tf_op jit(solution)/shard_map/ppermute | solution.py:154
  72.1 0.0 collective-permute-done.5.__.refs_1_
  72.1 0.0 all-to-all-done
  72.1 1.4 spread_classes.1
  73.5 8.3 %all-to-all-start.1 = ((f32[32,64,128]{2,1,0:T(8,128)}), f32[32,64,128]{2,1,0:T(8,128)S(1)}, u32[]{:S(2)}, u32[]{:S(2)}) async-start(f32[32,64,128]{2,1,0:T(8,128)} %bitcast.10), calls=%async_computation.1 | async-start | bytes 2097152 | tf_op jit(solution)/shard_map/all_to_all | solution.py:166
  81.9 1.9 %collective-permute-start.6 = (f32[8,4,16,128]{3,2,1,0:T(8,128)S(1)}, f32[8,4,16,128]{3,2,1,0:T(8,128)S(1)}, u32[]{:S(2)}, u32[]{:S(2)}) collective-permute-start(f32[8,4,16,128]{3,2,1,0:T(8,128)S(1)} %collective-permute-done.4._.refs_2_), channel_id=1, source_target_pairs={{0,32},{32,0},{64,96},{96,64},{1,33},{33,1},{65,97},{97,65},{2,34}... | collective-permute-start | bytes 786440 | tf_op jit(solution)/shard_map/ppermute | solution.py:156
  83.8 0.2 convert_reduce_fusion
  84.0 0.6 fusion.12
  84.6 6.8 %collective-permute-done.6.refs_3_ = f32[8,4,16,128]{3,2,1,0:T(8,128)S(1)} collective-permute-done((f32[8,4,16,128]{3,2,1,0:T(8,128)S(1)}, f32[8,4,16,128]{3,2,1,0:T(8,128)S(1)}, u32[]{:S(2)}, u32[]{:S(2)}) %collective-permute-start.6) | collective-permute-done | bytes 262176 | tf_op jit(solution)/shard_map/ppermute | solution.py:156
  91.5 7.6 %all-to-all-done.1 = f32[32,64,128]{2,1,0:T(8,128)S(1)} async-done(((f32[32,64,128]{2,1,0:T(8,128)}), f32[32,64,128]{2,1,0:T(8,128)S(1)}, u32[]{:S(2)}, u32[]{:S(2)}) %all-to-all-start.1) | async-done | bytes 1048608 | tf_op jit(solution)/shard_map/all_to_all | solution.py:166
  99.1 2.3 %ladder_terms.1 = f32[512,128]{1,0:T(8,128)} custom-call(s32[1,128]{1,0:T(1,128)S(1)} %bitcast.37, f32[2048,128]{1,0:T(8,128)S(1)} %bitcast.31, f32[8,4,16,128]{3,2,1,0:T(8,128)S(1)} %pad_maximum_fusion.refs_0_, f32[8,4,16,128]{3,2,1,0:T(8,128)S(1)} %collective-permute-done.5.__.refs_1_, f32[8,4,16,128]{3,2,1,0:T(8,128)S(1)} %collective-permute-done.4._.refs_2_, ...), custom_call_target="tpu_custom_call" | custom-call | tf_op jit(solution)/shard_map/ladder_terms/pallas_call | solution.py:170
  101.4 3.9 %all-to-all-start.2 = ((f32[32,16,128]{2,1,0:T(8,128)}), f32[32,16,128]{2,1,0:T(8,128)S(1)}, u32[]{:S(2)}, u32[]{:S(2)}) async-start(f32[32,16,128]{2,1,0:T(8,128)} %bitcast.12), calls=%async_computation.2 | async-start | bytes 524288 | tf_op jit(solution)/shard_map/all_to_all | solution.py:179
  105.3 0.1 slice_bitcast_fusion.1
  105.4 0.1 fusion.13
  105.5 8.9 %all-to-all-done.2 = f32[32,16,128]{2,1,0:T(8,128)S(1)} async-done(((f32[32,16,128]{2,1,0:T(8,128)}), f32[32,16,128]{2,1,0:T(8,128)S(1)}, u32[]{:S(2)}, u32[]{:S(2)}) %all-to-all-start.2) | async-done | bytes 262176 | tf_op jit(solution)/shard_map/all_to_all | solution.py:179
  114.3 1.4 gather_fusion
  115.8 23.6 %all-to-all-start.3 = ((f32[128,4,128]{2,1,0:T(4,128)}), f32[128,4,128]{2,1,0:T(4,128)S(1)}, u32[]{:S(2)}, u32[]{:S(2)}) async-start(f32[128,4,128]{2,1,0:T(4,128)} %gather_fusion), calls=%async_computation.3 | async-start | bytes 524288 | tf_op jit(solution)/shard_map/all_to_all | solution.py:116
  139.3 0.0 copy-start.2
  142.0 0.0 copy-start.3
  142.0 0.0 copy-start.4
  142.0 21.8 %all-to-all-done.3 = f32[128,4,128]{2,1,0:T(4,128)S(1)} async-done(((f32[128,4,128]{2,1,0:T(4,128)}), f32[128,4,128]{2,1,0:T(4,128)S(1)}, u32[]{:S(2)}, u32[]{:S(2)}) %all-to-all-start.3) | async-done | bytes 262176 | tf_op jit(solution)/shard_map/all_to_all | solution.py:116
  163.8 0.0 copy-done.2
  163.8 0.0 copy-done.3
  163.8 0.0 copy-done.4
  163.8 0.7 fusion.9
  (4 shorter events, 0.1 us)
Async XLA Ops:
  1.5 33.4 %copy-start = (f32[1,32,16,128]{3,2,1,0:T(8,128)S(1)}, f32[1,32,16,128]{3,2,1,0:T(8,128)}, u32[]{:S(2)}) copy-start(f32[1,32,16,128]{3,2,1,0:T(8,128)} %param.7) | copy-start | bytes 786436
  1.5 70.6 %all-to-all-start = ((f32[128,4,128]{2,1,0:T(4,128)}), f32[128,4,128]{2,1,0:T(4,128)S(1)}, u32[]{:S(2)}, u32[]{:S(2)}) async-start(f32[128,4,128]{2,1,0:T(4,128)} %bitcast.39), calls=%async_computation | async-start | bytes 524288 | tf_op jit(solution)/shard_map/all_to_all | solution.py:116
  34.9 0.7 copy-start.1
  35.7 4.1 %collective-permute-start = (f32[4,4,16,128]{3,2,1,0:T(8,128)S(1)}, f32[4,4,16,128]{3,2,1,0:T(8,128)S(1)}, u32[]{:S(2)}, u32[]{:S(2)}) collective-permute-start(f32[4,4,16,128]{3,2,1,0:T(8,128)S(1)} %get-tuple-element.8), channel_id=1, source_target_pairs={{0,1},{1,0},{2,3},{3,2},{4,5},{5,4},{6,7},{7,6},{8,9},{9,8},{10,11... | collective-permute-start | bytes 393224 | tf_op jit(solution)/shard_map/ppermute | solution.py:150
  39.8 9.0 %collective-permute-start.3 = (f32[2,4,16,128]{3,2,1,0:T(8,128)S(1)}, f32[2,4,16,128]{3,2,1,0:T(8,128)S(1)}, u32[]{:S(2)}, u32[]{:S(2)}) collective-permute-start(f32[2,4,16,128]{3,2,1,0:T(8,128)S(1)} %get-tuple-element.11), channel_id=1, source_target_pairs={{0,6},{2,4},{4,2},{6,0},{1,7},{3,5},{5,3},{7,1},{8,14},{10,12},{12... | collective-permute-start | bytes 196616 | tf_op jit(solution)/shard_map/ppermute | solution.py:152
  44.2 6.8 %collective-permute-start.2 = (f32[2,4,16,128]{3,2,1,0:T(8,128)S(1)}, f32[2,4,16,128]{3,2,1,0:T(8,128)S(1)}, u32[]{:S(2)}, u32[]{:S(2)}) collective-permute-start(f32[2,4,16,128]{3,2,1,0:T(8,128)S(1)} %get-tuple-element.12), channel_id=1, source_target_pairs={{0,4},{2,6},{4,0},{6,2},{1,5},{3,7},{5,1},{7,3},{8,12},{10,14},{12... | collective-permute-start | bytes 196616 | tf_op jit(solution)/shard_map/ppermute | solution.py:152
  46.6 5.3 %collective-permute-start.1 = (f32[2,4,16,128]{3,2,1,0:T(8,128)S(1)}, f32[2,4,16,128]{3,2,1,0:T(8,128)S(1)}, u32[]{:S(2)}, u32[]{:S(2)}) collective-permute-start(f32[2,4,16,128]{3,2,1,0:T(8,128)S(1)} %get-tuple-element.10), channel_id=1, source_target_pairs={{0,2},{2,0},{4,6},{6,4},{1,3},{3,1},{5,7},{7,5},{8,10},{10,8},{12,... | collective-permute-start | bytes 196616 | tf_op jit(solution)/shard_map/ppermute | solution.py:152
  52.0 20.1 %collective-permute-start.4 = (f32[8,4,16,128]{3,2,1,0:T(8,128)S(1)}, f32[8,4,16,128]{3,2,1,0:T(8,128)S(1)}, u32[]{:S(2)}, u32[]{:S(2)}) collective-permute-start(f32[8,4,16,128]{3,2,1,0:T(8,128)S(1)} %pad_maximum_fusion.refs_0_), channel_id=1, source_target_pairs={{0,64},{32,96},{64,0},{96,32},{1,65},{33,97},{65,1},{97,33},{2,66}... | collective-permute-start | bytes 786440 | tf_op jit(solution)/shard_map/ppermute | solution.py:154
  56.0 16.1 %collective-permute-start.5 = (f32[8,4,16,128]{3,2,1,0:T(8,128)S(1)}, f32[8,4,16,128]{3,2,1,0:T(8,128)S(1)}, u32[]{:S(2)}, u32[]{:S(2)}) collective-permute-start(f32[8,4,16,128]{3,2,1,0:T(8,128)S(1)} %pad_maximum_fusion.refs_0_), channel_id=1, source_target_pairs={{0,32},{32,0},{64,96},{96,64},{1,33},{33,1},{65,97},{97,65},{2,34}... | collective-permute-start | bytes 786440 | tf_op jit(solution)/shard_map/ppermute | solution.py:155
  73.5 25.5 %all-to-all-start.1 = ((f32[32,64,128]{2,1,0:T(8,128)}), f32[32,64,128]{2,1,0:T(8,128)S(1)}, u32[]{:S(2)}, u32[]{:S(2)}) async-start(f32[32,64,128]{2,1,0:T(8,128)} %bitcast.10), calls=%async_computation.1 | async-start | bytes 2097152 | tf_op jit(solution)/shard_map/all_to_all | solution.py:166
  81.9 9.6 %collective-permute-start.6 = (f32[8,4,16,128]{3,2,1,0:T(8,128)S(1)}, f32[8,4,16,128]{3,2,1,0:T(8,128)S(1)}, u32[]{:S(2)}, u32[]{:S(2)}) collective-permute-start(f32[8,4,16,128]{3,2,1,0:T(8,128)S(1)} %collective-permute-done.4._.refs_2_), channel_id=1, source_target_pairs={{0,32},{32,0},{64,96},{96,64},{1,33},{33,1},{65,97},{97,65},{2,34}... | collective-permute-start | bytes 786440 | tf_op jit(solution)/shard_map/ppermute | solution.py:156
  101.4 12.9 %all-to-all-start.2 = ((f32[32,16,128]{2,1,0:T(8,128)}), f32[32,16,128]{2,1,0:T(8,128)S(1)}, u32[]{:S(2)}, u32[]{:S(2)}) async-start(f32[32,16,128]{2,1,0:T(8,128)} %bitcast.12), calls=%async_computation.2 | async-start | bytes 524288 | tf_op jit(solution)/shard_map/all_to_all | solution.py:179
  115.8 48.0 %all-to-all-start.3 = ((f32[128,4,128]{2,1,0:T(4,128)}), f32[128,4,128]{2,1,0:T(4,128)S(1)}, u32[]{:S(2)}, u32[]{:S(2)}) async-start(f32[128,4,128]{2,1,0:T(4,128)} %gather_fusion), calls=%async_computation.3 | async-start | bytes 524288 | tf_op jit(solution)/shard_map/all_to_all | solution.py:116
  139.3 24.5 %copy-start.2 = (f32[64,128]{1,0:T(8,128)S(1)}, f32[64,128]{1,0:T(8,128)}, u32[]{:S(2)}) copy-start(f32[64,128]{1,0:T(8,128)} %param.8) | copy-start | bytes 98308
  142.0 21.8 %copy-start.3 = (f32[64]{0:T(128)S(1)}, f32[64]{0:T(128)}, u32[]{:S(2)}) copy-start(f32[64]{0:T(128)} %param.9) | copy-start | bytes 772
  142.0 21.8 %copy-start.4 = (f32[128]{0:T(128)S(1)}, f32[128]{0:T(128)}, u32[]{:S(2)}) copy-start(f32[128]{0:T(128)} %param.10) | copy-start | bytes 1540

commit v3 on v2

--- a/solution.py
+++ b/solution.py
@@ -58,7 +58,7 @@
                 out_ref[d, turn] = integrals_ref[turn * CLASSES + slot]
 
 
-def spread_kernel(irreps_ref, blocks_ref, _, __, out_ref, *, share):
+def spread_kernel(irreps_ref, blocks_ref, _, out_ref, *, share):
     blocks = irreps_ref.shape[1]
     held = blocks // CLASSES
     row = lax.broadcasted_iota(jnp.int32, (blocks, blocks), 0)
@@ -158,11 +158,11 @@
     by_class = pl.pallas_call(
         functools.partial(spread_kernel, share=share),
         out_shape=jax.ShapeDtypeStruct((Y, CLASSES, share * held, width), jnp.float32),
-        in_specs=[WHOLE, WHOLE] + [pl.BlockSpec(memory_space=pl.ANY)] * 2,
+        in_specs=[WHOLE, WHOLE, pl.BlockSpec(memory_space=pl.ANY)],
         out_specs=WHOLE,
         compiler_params=pltpu.CompilerParams(vmem_limit_bytes=24 * 1024 * 1024),
         name="spread_classes",
-    )(irreps, spread.reshape(share * blocks, width), far, near)
+    )(irreps, spread.reshape(share * blocks, width), far)
     by_class = lax.all_to_all(
         by_class.reshape(sources, share * held, width), PLANE, split_axis=0, concat_axis=0, tiled=True
     )

time: 165 us -> 168 us (1.018)
  starting transfers between devices: 90.4 us -> 93.4 us
    all_to_all x1, waiting for transfers between devices: 7.61 us -> 1.99 us  [per_device(): lax.all_to_all(by_class.reshape(sources, share * held, width), PLANE, spl...]
    ppermute x1, waiting for transfers between devices: 0.01 us -> 3.45 us  [per_device(): near = lax.ppermute(own, 'l', [(i, i ^ 1) for i in range(LO)])]
    ppermute x1, waiting for transfers between devices: 13 us -> 16.1 us  [per_device(): far = lax.ppermute(own, 'l', [(i, i ^ 2) for i in range(LO)])]
    all_to_all x1, starting transfers between devices: 3.91 us -> 6.08 us  [per_device(): lax.all_to_all(partial.reshape(sources, share * LO, width), PLANE, split_...]
  transfers between devices with their start and end apart: 11 -> 11, of which waited for: 8 -> 9; matrix products, arithmetic and copies ran while one was open for 1% -> 1% of each run, Pallas kernels for 0% -> 0%
where the time goes in v3:
time: 168 us; the launch traced here: 167 us
  starting transfers between devices  93.4 us (56%)
  waiting for transfers between devices  61.8 us (37%)
  Pallas kernels  5.37 us (3%)
  between operations  2.81 us (2%)
  local copies, waits for them, and re-layouts  2.17 us (1%)
    all_to_all x2, starting transfers between devices, exchange(): lax.all_to_all(pieces, VP, split_axis=0, concat_axis=0, tiled=True, axis_...  58 us
    all_to_all x2, waiting for transfers between devices, exchange(): lax.all_to_all(pieces, VP, split_axis=0, concat_axis=0, tiled=True, axis_...  21.8 us
    ppermute x1, waiting for transfers between devices, per_device(): far = lax.ppermute(own, 'l', [(i, i ^ 2) for i in range(LO)])  16.1 us
    ppermute x3, starting transfers between devices, per_device(): lax.ppermute(cores[d], 'x', [(i, i ^ d) for i in range(X)])  8.98 us
    all_to_all x1, waiting for transfers between devices, per_device(): lax.all_to_all(partial.reshape(sources, share * LO, width), PLANE, split_...  8.74 us
    all_to_all x1, starting transfers between devices, per_device(): lax.all_to_all(by_class.reshape(sources, share * held, width), PLANE, spl...  7.83 us
    all_to_all x1, starting transfers between devices, per_device(): lax.all_to_all(partial.reshape(sources, share * LO, width), PLANE, split_...  6.08 us
    ppermute x1, waiting for transfers between devices, per_device(): lax.ppermute(far, 'l', [(i, i ^ 1) for i in range(LO)])  5.62 us
  transfers between devices with their start and end apart: 11, of which 9 were waited for; matrix products, arithmetic and copies ran while one was open for 1% of the time, Pallas kernels for 0%

profile of v3, /device:TPU:1, one launch (start us, length us, event | category | flops | bytes accessed | tf_op | source)
XLA Modules:
  0.0 167.1 jit_solution(7280756082492257519)
XLA Ops:
  0.0 1.5 copy_rows.1
  1.5 0.0 copy-start
  1.5 33.4 %all-to-all-start = ((f32[128,4,128]{2,1,0:T(4,128)}), f32[128,4,128]{2,1,0:T(4,128)S(1)}, u32[]{:S(2)}, u32[]{:S(2)}) async-start(f32[128,4,128]{2,1,0:T(4,128)} %bitcast.39), calls=%async_computation | async-start | bytes 524288 | tf_op jit(solution)/shard_map/all_to_all | solution.py:116
  34.9 0.0 copy-start.1
  34.9 0.0 copy-done
  34.9 0.6 copy-done.1
  35.5 0.1 roll_slots.1
  35.7 3.1 %collective-permute-start = (f32[4,4,16,128]{3,2,1,0:T(8,128)S(1)}, f32[4,4,16,128]{3,2,1,0:T(8,128)S(1)}, u32[]{:S(2)}, u32[]{:S(2)}) collective-permute-start(f32[4,4,16,128]{3,2,1,0:T(8,128)S(1)} %get-tuple-element.8), channel_id=1, source_target_pairs={{0,1},{1,0},{2,3},{3,2},{4,5},{5,4},{6,7},{7,6},{8,9},{9,8},{10,11... | collective-permute-start | bytes 393224 | tf_op jit(solution)/shard_map/ppermute | solution.py:150
  38.8 1.0 collective-permute-done
  39.8 4.4 %collective-permute-start.3 = (f32[2,4,16,128]{3,2,1,0:T(8,128)S(1)}, f32[2,4,16,128]{3,2,1,0:T(8,128)S(1)}, u32[]{:S(2)}, u32[]{:S(2)}) collective-permute-start(f32[2,4,16,128]{3,2,1,0:T(8,128)S(1)} %get-tuple-element.11), channel_id=1, source_target_pairs={{0,6},{2,4},{4,2},{6,0},{1,7},{3,5},{5,3},{7,1},{8,14},{10,12},{12... | collective-permute-start | bytes 196616 | tf_op jit(solution)/shard_map/ppermute | solution.py:152
  44.2 2.4 %collective-permute-start.2 = (f32[2,4,16,128]{3,2,1,0:T(8,128)S(1)}, f32[2,4,16,128]{3,2,1,0:T(8,128)S(1)}, u32[]{:S(2)}, u32[]{:S(2)}) collective-permute-start(f32[2,4,16,128]{3,2,1,0:T(8,128)S(1)} %get-tuple-element.12), channel_id=1, source_target_pairs={{0,4},{2,6},{4,0},{6,2},{1,5},{3,7},{5,1},{7,3},{8,12},{10,14},{12... | collective-permute-start | bytes 196616 | tf_op jit(solution)/shard_map/ppermute | solution.py:152
  46.6 2.2 %collective-permute-start.1 = (f32[2,4,16,128]{3,2,1,0:T(8,128)S(1)}, f32[2,4,16,128]{3,2,1,0:T(8,128)S(1)}, u32[]{:S(2)}, u32[]{:S(2)}) collective-permute-start(f32[2,4,16,128]{3,2,1,0:T(8,128)S(1)} %get-tuple-element.10), channel_id=1, source_target_pairs={{0,2},{2,0},{4,6},{6,4},{1,3},{3,1},{5,7},{7,5},{8,10},{10,8},{12,... | collective-permute-start | bytes 196616 | tf_op jit(solution)/shard_map/ppermute | solution.py:152
  48.8 0.0 collective-permute-done.3
  48.8 2.2 %collective-permute-done.2 = f32[2,4,16,128]{3,2,1,0:T(8,128)S(1)} collective-permute-done((f32[2,4,16,128]{3,2,1,0:T(8,128)S(1)}, f32[2,4,16,128]{3,2,1,0:T(8,128)S(1)}, u32[]{:S(2)}, u32[]{:S(2)}) %collective-permute-start.2) | collective-permute-done | bytes 65568 | tf_op jit(solution)/shard_map/ppermute | solution.py:152
  51.0 0.9 collective-permute-done.1
  52.0 4.0 %collective-permute-start.4 = (f32[8,4,16,128]{3,2,1,0:T(8,128)S(1)}, f32[8,4,16,128]{3,2,1,0:T(8,128)S(1)}, u32[]{:S(2)}, u32[]{:S(2)}) collective-permute-start(f32[8,4,16,128]{3,2,1,0:T(8,128)S(1)} %pad_maximum_fusion.refs_0_), channel_id=1, source_target_pairs={{0,64},{32,96},{64,0},{96,32},{1,65},{33,97},{65,1},{97,33},{2,66}... | collective-permute-start | bytes 786440 | tf_op jit(solution)/shard_map/ppermute | solution.py:154
  56.0 16.1 %collective-permute-done.4._.refs_2_ = f32[8,4,16,128]{3,2,1,0:T(8,128)S(1)} collective-permute-done((f32[8,4,16,128]{3,2,1,0:T(8,128)S(1)}, f32[8,4,16,128]{3,2,1,0:T(8,128)S(1)}, u32[]{:S(2)}, u32[]{:S(2)}) %collective-permute-start.4) | collective-permute-done | bytes 262176 | tf_op jit(solution)/shard_map/ppermute | solution.py:154
  72.1 0.0 all-to-all-done
  72.1 1.4 spread_classes.1
  73.5 7.8 %all-to-all-start.1 = ((f32[32,64,128]{2,1,0:T(8,128)}), f32[32,64,128]{2,1,0:T(8,128)S(1)}, u32[]{:S(2)}, u32[]{:S(2)}) async-start(f32[32,64,128]{2,1,0:T(8,128)} %bitcast.10), calls=%async_computation.1 | async-start | bytes 2097152 | tf_op jit(solution)/shard_map/all_to_all | solution.py:166
  81.4 1.9 %collective-permute-start.5 = (f32[8,4,16,128]{3,2,1,0:T(8,128)S(1)}, f32[8,4,16,128]{3,2,1,0:T(8,128)S(1)}, u32[]{:S(2)}, u32[]{:S(2)}) collective-permute-start(f32[8,4,16,128]{3,2,1,0:T(8,128)S(1)} %pad_maximum_fusion.refs_0_), channel_id=1, source_target_pairs={{0,32},{32,0},{64,96},{96,64},{1,33},{33,1},{65,97},{97,65},{2,34}... | collective-permute-start | bytes 786440 | tf_op jit(solution)/shard_map/ppermute | solution.py:155
  83.3 3.4 %collective-permute-start.6 = (f32[8,4,16,128]{3,2,1,0:T(8,128)S(1)}, f32[8,4,16,128]{3,2,1,0:T(8,128)S(1)}, u32[]{:S(2)}, u32[]{:S(2)}) collective-permute-start(f32[8,4,16,128]{3,2,1,0:T(8,128)S(1)} %collective-permute-done.4._.refs_2_), channel_id=1, source_target_pairs={{0,32},{32,0},{64,96},{96,64},{1,33},{33,1},{65,97},{97,65},{2,34}... | collective-permute-start | bytes 786440 | tf_op jit(solution)/shard_map/ppermute | solution.py:156
  86.7 0.2 convert_reduce_fusion
  86.9 0.6 fusion.12
  87.5 3.4 %collective-permute-done.5.refs_1_ = f32[8,4,16,128]{3,2,1,0:T(8,128)S(1)} collective-permute-done((f32[8,4,16,128]{3,2,1,0:T(8,128)S(1)}, f32[8,4,16,128]{3,2,1,0:T(8,128)S(1)}, u32[]{:S(2)}, u32[]{:S(2)}) %collective-permute-start.5) | collective-permute-done | bytes 262176 | tf_op jit(solution)/shard_map/ppermute | solution.py:155
  90.9 5.6 %collective-permute-done.6.refs_3_ = f32[8,4,16,128]{3,2,1,0:T(8,128)S(1)} collective-permute-done((f32[8,4,16,128]{3,2,1,0:T(8,128)S(1)}, f32[8,4,16,128]{3,2,1,0:T(8,128)S(1)}, u32[]{:S(2)}, u32[]{:S(2)}) %collective-permute-start.6) | collective-permute-done | bytes 262176 | tf_op jit(solution)/shard_map/ppermute | solution.py:156
  96.6 2.0 %all-to-all-done.1 = f32[32,64,128]{2,1,0:T(8,128)S(1)} async-done(((f32[32,64,128]{2,1,0:T(8,128)}), f32[32,64,128]{2,1,0:T(8,128)S(1)}, u32[]{:S(2)}, u32[]{:S(2)}) %all-to-all-start.1) | async-done | bytes 1048608 | tf_op jit(solution)/shard_map/all_to_all | solution.py:166
  98.5 2.3 %ladder_terms.1 = f32[512,128]{1,0:T(8,128)} custom-call(s32[1,128]{1,0:T(1,128)S(1)} %bitcast.37, f32[2048,128]{1,0:T(8,128)S(1)} %bitcast.31, f32[8,4,16,128]{3,2,1,0:T(8,128)S(1)} %pad_maximum_fusion.refs_0_, f32[8,4,16,128]{3,2,1,0:T(8,128)S(1)} %collective-permute-done.5.refs_1_, f32[8,4,16,128]{3,2,1,0:T(8,128)S(1)} %collective-permute-done.4._.refs_2_, ...), custom_call_target="tpu_custom_call" | custom-call | tf_op jit(solution)/shard_map/ladder_terms/pallas_call | solution.py:170
  100.9 6.1 %all-to-all-start.2 = ((f32[32,16,128]{2,1,0:T(8,128)}), f32[32,16,128]{2,1,0:T(8,128)S(1)}, u32[]{:S(2)}, u32[]{:S(2)}) async-start(f32[32,16,128]{2,1,0:T(8,128)} %bitcast.12), calls=%async_computation.2 | async-start | bytes 524288 | tf_op jit(solution)/shard_map/all_to_all | solution.py:179
  107.0 0.1 slice_bitcast_fusion.1
  107.0 0.1 fusion.13
  107.1 8.7 %all-to-all-done.2 = f32[32,16,128]{2,1,0:T(8,128)S(1)} async-done(((f32[32,16,128]{2,1,0:T(8,128)}), f32[32,16,128]{2,1,0:T(8,128)S(1)}, u32[]{:S(2)}, u32[]{:S(2)}) %all-to-all-start.2) | async-done | bytes 262176 | tf_op jit(solution)/shard_map/all_to_all | solution.py:179
  115.9 1.4 gather_fusion
  117.3 24.6 %all-to-all-start.3 = ((f32[128,4,128]{2,1,0:T(4,128)}), f32[128,4,128]{2,1,0:T(4,128)S(1)}, u32[]{:S(2)}, u32[]{:S(2)}) async-start(f32[128,4,128]{2,1,0:T(4,128)} %gather_fusion), calls=%async_computation.3 | async-start | bytes 524288 | tf_op jit(solution)/shard_map/all_to_all | solution.py:116
  141.9 0.0 copy-start.2
  144.6 0.0 copy-start.3
  144.6 0.0 copy-start.4
  144.6 21.8 %all-to-all-done.3 = f32[128,4,128]{2,1,0:T(4,128)S(1)} async-done(((f32[128,4,128]{2,1,0:T(4,128)}), f32[128,4,128]{2,1,0:T(4,128)S(1)}, u32[]{:S(2)}, u32[]{:S(2)}) %all-to-all-start.3) | async-done | bytes 262176 | tf_op jit(solution)/shard_map/all_to_all | solution.py:116
  166.4 0.0 copy-done.2
  166.4 0.0 copy-done.3
  166.4 0.0 copy-done.4
  166.4 0.7 fusion.9
  (4 shorter events, 0.1 us)
Async XLA Ops:
  1.5 33.4 %copy-start = (f32[1,32,16,128]{3,2,1,0:T(8,128)S(1)}, f32[1,32,16,128]{3,2,1,0:T(8,128)}, u32[]{:S(2)}) copy-start(f32[1,32,16,128]{3,2,1,0:T(8,128)} %param.7) | copy-start | bytes 786436
  1.5 70.6 %all-to-all-start = ((f32[128,4,128]{2,1,0:T(4,128)}), f32[128,4,128]{2,1,0:T(4,128)S(1)}, u32[]{:S(2)}, u32[]{:S(2)}) async-start(f32[128,4,128]{2,1,0:T(4,128)} %bitcast.39), calls=%async_computation | async-start | bytes 524288 | tf_op jit(solution)/shard_map/all_to_all | solution.py:116
  34.9 0.7 copy-start.1
  35.7 4.1 %collective-permute-start = (f32[4,4,16,128]{3,2,1,0:T(8,128)S(1)}, f32[4,4,16,128]{3,2,1,0:T(8,128)S(1)}, u32[]{:S(2)}, u32[]{:S(2)}) collective-permute-start(f32[4,4,16,128]{3,2,1,0:T(8,128)S(1)} %get-tuple-element.8), channel_id=1, source_target_pairs={{0,1},{1,0},{2,3},{3,2},{4,5},{5,4},{6,7},{7,6},{8,9},{9,8},{10,11... | collective-permute-start | bytes 393224 | tf_op jit(solution)/shard_map/ppermute | solution.py:150
  39.8 9.0 %collective-permute-start.3 = (f32[2,4,16,128]{3,2,1,0:T(8,128)S(1)}, f32[2,4,16,128]{3,2,1,0:T(8,128)S(1)}, u32[]{:S(2)}, u32[]{:S(2)}) collective-permute-start(f32[2,4,16,128]{3,2,1,0:T(8,128)S(1)} %get-tuple-element.11), channel_id=1, source_target_pairs={{0,6},{2,4},{4,2},{6,0},{1,7},{3,5},{5,3},{7,1},{8,14},{10,12},{12... | collective-permute-start | bytes 196616 | tf_op jit(solution)/shard_map/ppermute | solution.py:152
  44.2 6.8 %collective-permute-start.2 = (f32[2,4,16,128]{3,2,1,0:T(8,128)S(1)}, f32[2,4,16,128]{3,2,1,0:T(8,128)S(1)}, u32[]{:S(2)}, u32[]{:S(2)}) collective-permute-start(f32[2,4,16,128]{3,2,1,0:T(8,128)S(1)} %get-tuple-element.12), channel_id=1, source_target_pairs={{0,4},{2,6},{4,0},{6,2},{1,5},{3,7},{5,1},{7,3},{8,12},{10,14},{12... | collective-permute-start | bytes 196616 | tf_op jit(solution)/shard_map/ppermute | solution.py:152
  46.6 5.3 %collective-permute-start.1 = (f32[2,4,16,128]{3,2,1,0:T(8,128)S(1)}, f32[2,4,16,128]{3,2,1,0:T(8,128)S(1)}, u32[]{:S(2)}, u32[]{:S(2)}) collective-permute-start(f32[2,4,16,128]{3,2,1,0:T(8,128)S(1)} %get-tuple-element.10), channel_id=1, source_target_pairs={{0,2},{2,0},{4,6},{6,4},{1,3},{3,1},{5,7},{7,5},{8,10},{10,8},{12,... | collective-permute-start | bytes 196616 | tf_op jit(solution)/shard_map/ppermute | solution.py:152
  52.0 20.1 %collective-permute-start.4 = (f32[8,4,16,128]{3,2,1,0:T(8,128)S(1)}, f32[8,4,16,128]{3,2,1,0:T(8,128)S(1)}, u32[]{:S(2)}, u32[]{:S(2)}) collective-permute-start(f32[8,4,16,128]{3,2,1,0:T(8,128)S(1)} %pad_maximum_fusion.refs_0_), channel_id=1, source_target_pairs={{0,64},{32,96},{64,0},{96,32},{1,65},{33,97},{65,1},{97,33},{2,66}... | collective-permute-start | bytes 786440 | tf_op jit(solution)/shard_map/ppermute | solution.py:154
  73.5 25.0 %all-to-all-start.1 = ((f32[32,64,128]{2,1,0:T(8,128)}), f32[32,64,128]{2,1,0:T(8,128)S(1)}, u32[]{:S(2)}, u32[]{:S(2)}) async-start(f32[32,64,128]{2,1,0:T(8,128)} %bitcast.10), calls=%async_computation.1 | async-start | bytes 2097152 | tf_op jit(solution)/shard_map/all_to_all | solution.py:166
  81.4 9.6 %collective-permute-start.5 = (f32[8,4,16,128]{3,2,1,0:T(8,128)S(1)}, f32[8,4,16,128]{3,2,1,0:T(8,128)S(1)}, u32[]{:S(2)}, u32[]{:S(2)}) collective-permute-start(f32[8,4,16,128]{3,2,1,0:T(8,128)S(1)} %pad_maximum_fusion.refs_0_), channel_id=1, source_target_pairs={{0,32},{32,0},{64,96},{96,64},{1,33},{33,1},{65,97},{97,65},{2,34}... | collective-permute-start | bytes 786440 | tf_op jit(solution)/shard_map/ppermute | solution.py:155
  83.3 13.3 %collective-permute-start.6 = (f32[8,4,16,128]{3,2,1,0:T(8,128)S(1)}, f32[8,4,16,128]{3,2,1,0:T(8,128)S(1)}, u32[]{:S(2)}, u32[]{:S(2)}) collective-permute-start(f32[8,4,16,128]{3,2,1,0:T(8,128)S(1)} %collective-permute-done.4._.refs_2_), channel_id=1, source_target_pairs={{0,32},{32,0},{64,96},{96,64},{1,33},{33,1},{65,97},{97,65},{2,34}... | collective-permute-start | bytes 786440 | tf_op jit(solution)/shard_map/ppermute | solution.py:156
  100.9 15.0 %all-to-all-start.2 = ((f32[32,16,128]{2,1,0:T(8,128)}), f32[32,16,128]{2,1,0:T(8,128)S(1)}, u32[]{:S(2)}, u32[]{:S(2)}) async-start(f32[32,16,128]{2,1,0:T(8,128)} %bitcast.12), calls=%async_computation.2 | async-start | bytes 524288 | tf_op jit(solution)/shard_map/all_to_all | solution.py:179
  117.3 49.1 %all-to-all-start.3 = ((f32[128,4,128]{2,1,0:T(4,128)}), f32[128,4,128]{2,1,0:T(4,128)S(1)}, u32[]{:S(2)}, u32[]{:S(2)}) async-start(f32[128,4,128]{2,1,0:T(4,128)} %gather_fusion), calls=%async_computation.3 | async-start | bytes 524288 | tf_op jit(solution)/shard_map/all_to_all | solution.py:116
  141.9 24.5 %copy-start.2 = (f32[64,128]{1,0:T(8,128)S(1)}, f32[64,128]{1,0:T(8,128)}, u32[]{:S(2)}) copy-start(f32[64,128]{1,0:T(8,128)} %param.8) | copy-start | bytes 98308
  144.6 21.8 %copy-start.3 = (f32[64]{0:T(128)S(1)}, f32[64]{0:T(128)}, u32[]{:S(2)}) copy-start(f32[64]{0:T(128)} %param.9) | copy-start | bytes 772
  144.6 21.8 %copy-start.4 = (f32[128]{0:T(128)S(1)}, f32[128]{0:T(128)}, u32[]{:S(2)}) copy-start(f32[128]{0:T(128)} %param.10) | copy-start | bytes 1540

commit v4 on v2

--- a/solution.py
+++ b/solution.py
@@ -13,7 +13,7 @@
 VP = ("h", "l", "y")
 OP = ("x", "c")
 PLANE = ("y", "x", "c")
-OUT_FIRST, HOME_FIRST = 24, 16
+OUT_FIRST, HOME_FIRST = 24, 20
 WHOLE = pl.BlockSpec(memory_space=pltpu.VMEM)
 
 

time: 165 us -> 169 us (1.024)
  waiting for transfers between devices: 62.1 us -> 65.9 us
    all_to_all x2, waiting for transfers between devices: 21.8 us -> 25.5 us  [exchange(): lax.all_to_all(pieces, VP, split_axis=0, concat_axis=0, tiled=True, axis_...]
where the time goes in v4:
time: 169 us; the launch traced here: 168 us
  starting transfers between devices  90.1 us (53%)
  waiting for transfers between devices  65.9 us (39%)
  Pallas kernels  5.38 us (3%)
  between operations  2.82 us (2%)
  local copies, waits for them, and re-layouts  2.18 us (1%)
    all_to_all x2, starting transfers between devices, exchange(): lax.all_to_all(pieces, VP, split_axis=0, concat_axis=0, tiled=True, axis_...  56.7 us
    all_to_all x2, waiting for transfers between devices, exchange(): lax.all_to_all(pieces, VP, split_axis=0, concat_axis=0, tiled=True, axis_...  25.5 us
    ppermute x1, waiting for transfers between devices, per_device(): far = lax.ppermute(own, 'l', [(i, i ^ 2) for i in range(LO)])  13 us
    ppermute x3, starting transfers between devices, per_device(): lax.ppermute(cores[d], 'x', [(i, i ^ d) for i in range(X)])  8.98 us
    all_to_all x1, waiting for transfers between devices, per_device(): lax.all_to_all(partial.reshape(sources, share * LO, width), PLANE, split_...  8.85 us
    all_to_all x1, starting transfers between devices, per_device(): lax.all_to_all(by_class.reshape(sources, share * held, width), PLANE, spl...  8.35 us
    all_to_all x1, waiting for transfers between devices, per_device(): lax.all_to_all(by_class.reshape(sources, share * held, width), PLANE, spl...  7.42 us
    ppermute x1, waiting for transfers between devices, per_device(): lax.ppermute(far, 'l', [(i, i ^ 1) for i in range(LO)])  7 us
  transfers between devices with their start and end apart: 11, of which 8 were waited for; matrix products, arithmetic and copies ran while one was open for 1% of the time, Pallas kernels for 0%

profile of v4, /device:TPU:1, one launch (start us, length us, event | category | flops | bytes accessed | tf_op | source)
XLA Modules:
  0.0 168.0 jit_solution(8150543590913937259)
XLA Ops:
  0.0 1.5 copy_rows.1
  1.5 0.0 copy-start
  1.5 33.4 %all-to-all-start = ((f32[128,4,128]{2,1,0:T(4,128)}), f32[128,4,128]{2,1,0:T(4,128)S(1)}, u32[]{:S(2)}, u32[]{:S(2)}) async-start(f32[128,4,128]{2,1,0:T(4,128)} %bitcast.39), calls=%async_computation | async-start | bytes 524288 | tf_op jit(solution)/shard_map/all_to_all | solution.py:116
  34.9 0.0 copy-start.1
  34.9 0.0 copy-done
  34.9 0.6 copy-done.1
  35.5 0.1 roll_slots.1
  35.7 3.1 %collective-permute-start = (f32[4,4,16,128]{3,2,1,0:T(8,128)S(1)}, f32[4,4,16,128]{3,2,1,0:T(8,128)S(1)}, u32[]{:S(2)}, u32[]{:S(2)}) collective-permute-start(f32[4,4,16,128]{3,2,1,0:T(8,128)S(1)} %get-tuple-element.8), channel_id=1, source_target_pairs={{0,1},{1,0},{2,3},{3,2},{4,5},{5,4},{6,7},{7,6},{8,9},{9,8},{10,11... | collective-permute-start | bytes 393224 | tf_op jit(solution)/shard_map/ppermute | solution.py:150
  38.8 1.0 collective-permute-done
  39.8 4.4 %collective-permute-start.3 = (f32[2,4,16,128]{3,2,1,0:T(8,128)S(1)}, f32[2,4,16,128]{3,2,1,0:T(8,128)S(1)}, u32[]{:S(2)}, u32[]{:S(2)}) collective-permute-start(f32[2,4,16,128]{3,2,1,0:T(8,128)S(1)} %get-tuple-element.11), channel_id=1, source_target_pairs={{0,6},{2,4},{4,2},{6,0},{1,7},{3,5},{5,3},{7,1},{8,14},{10,12},{12... | collective-permute-start | bytes 196616 | tf_op jit(solution)/shard_map/ppermute | solution.py:152
  44.2 2.4 %collective-permute-start.2 = (f32[2,4,16,128]{3,2,1,0:T(8,128)S(1)}, f32[2,4,16,128]{3,2,1,0:T(8,128)S(1)}, u32[]{:S(2)}, u32[]{:S(2)}) collective-permute-start(f32[2,4,16,128]{3,2,1,0:T(8,128)S(1)} %get-tuple-element.12), channel_id=1, source_target_pairs={{0,4},{2,6},{4,0},{6,2},{1,5},{3,7},{5,1},{7,3},{8,12},{10,14},{12... | collective-permute-start | bytes 196616 | tf_op jit(solution)/shard_map/ppermute | solution.py:152
  46.6 2.2 %collective-permute-start.1 = (f32[2,4,16,128]{3,2,1,0:T(8,128)S(1)}, f32[2,4,16,128]{3,2,1,0:T(8,128)S(1)}, u32[]{:S(2)}, u32[]{:S(2)}) collective-permute-start(f32[2,4,16,128]{3,2,1,0:T(8,128)S(1)} %get-tuple-element.10), channel_id=1, source_target_pairs={{0,2},{2,0},{4,6},{6,4},{1,3},{3,1},{5,7},{7,5},{8,10},{10,8},{12,... | collective-permute-start | bytes 196616 | tf_op jit(solution)/shard_map/ppermute | solution.py:152
  48.8 0.0 collective-permute-done.3
  48.8 2.2 %collective-permute-done.2 = f32[2,4,16,128]{3,2,1,0:T(8,128)S(1)} collective-permute-done((f32[2,4,16,128]{3,2,1,0:T(8,128)S(1)}, f32[2,4,16,128]{3,2,1,0:T(8,128)S(1)}, u32[]{:S(2)}, u32[]{:S(2)}) %collective-permute-start.2) | collective-permute-done | bytes 65568 | tf_op jit(solution)/shard_map/ppermute | solution.py:152
  51.0 0.9 collective-permute-done.1
  52.0 4.0 %collective-permute-start.4 = (f32[8,4,16,128]{3,2,1,0:T(8,128)S(1)}, f32[8,4,16,128]{3,2,1,0:T(8,128)S(1)}, u32[]{:S(2)}, u32[]{:S(2)}) collective-permute-start(f32[8,4,16,128]{3,2,1,0:T(8,128)S(1)} %pad_maximum_fusion.refs_0_), channel_id=1, source_target_pairs={{0,64},{32,96},{64,0},{96,32},{1,65},{33,97},{65,1},{97,33},{2,66}... | collective-permute-start | bytes 786440 | tf_op jit(solution)/shard_map/ppermute | solution.py:154
  56.0 3.1 %collective-permute-start.5 = (f32[8,4,16,128]{3,2,1,0:T(8,128)S(1)}, f32[8,4,16,128]{3,2,1,0:T(8,128)S(1)}, u32[]{:S(2)}, u32[]{:S(2)}) collective-permute-start(f32[8,4,16,128]{3,2,1,0:T(8,128)S(1)} %pad_maximum_fusion.refs_0_), channel_id=1, source_target_pairs={{0,32},{32,0},{64,96},{96,64},{1,33},{33,1},{65,97},{97,65},{2,34}... | collective-permute-start | bytes 786440 | tf_op jit(solution)/shard_map/ppermute | solution.py:155
  59.1 13.0 %collective-permute-done.4._.refs_2_ = f32[8,4,16,128]{3,2,1,0:T(8,128)S(1)} collective-permute-done((f32[8,4,16,128]{3,2,1,0:T(8,128)S(1)}, f32[8,4,16,128]{3,2,1,0:T(8,128)S(1)}, u32[]{:S(2)}, u32[]{:S(2)}) %collective-permute-start.4) | collective-permute-done | bytes 262176 | tf_op jit(solution)/shard_map/ppermute | solution.py:154
  72.1 0.0 collective-permute-done.5.__.refs_1_
  72.1 0.0 all-to-all-done
  72.1 1.4 spread_classes.1
  73.5 8.3 %all-to-all-start.1 = ((f32[32,64,128]{2,1,0:T(8,128)}), f32[32,64,128]{2,1,0:T(8,128)S(1)}, u32[]{:S(2)}, u32[]{:S(2)}) async-start(f32[32,64,128]{2,1,0:T(8,128)} %bitcast.10), calls=%async_computation.1 | async-start | bytes 2097152 | tf_op jit(solution)/shard_map/all_to_all | solution.py:166
  81.9 0.2 convert_reduce_fusion
  82.1 1.9 %collective-permute-start.6 = (f32[8,4,16,128]{3,2,1,0:T(8,128)S(1)}, f32[8,4,16,128]{3,2,1,0:T(8,128)S(1)}, u32[]{:S(2)}, u32[]{:S(2)}) collective-permute-start(f32[8,4,16,128]{3,2,1,0:T(8,128)S(1)} %collective-permute-done.4._.refs_2_), channel_id=1, source_target_pairs={{0,32},{32,0},{64,96},{96,64},{1,33},{33,1},{65,97},{97,65},{2,34}... | collective-permute-start | bytes 786440 | tf_op jit(solution)/shard_map/ppermute | solution.py:156
  84.0 0.6 fusion.12
  84.7 7.0 %collective-permute-done.6.refs_3_ = f32[8,4,16,128]{3,2,1,0:T(8,128)S(1)} collective-permute-done((f32[8,4,16,128]{3,2,1,0:T(8,128)S(1)}, f32[8,4,16,128]{3,2,1,0:T(8,128)S(1)}, u32[]{:S(2)}, u32[]{:S(2)}) %collective-permute-start.6) | collective-permute-done | bytes 262176 | tf_op jit(solution)/shard_map/ppermute | solution.py:156
  91.7 7.4 %all-to-all-done.1 = f32[32,64,128]{2,1,0:T(8,128)S(1)} async-done(((f32[32,64,128]{2,1,0:T(8,128)}), f32[32,64,128]{2,1,0:T(8,128)S(1)}, u32[]{:S(2)}, u32[]{:S(2)}) %all-to-all-start.1) | async-done | bytes 1048608 | tf_op jit(solution)/shard_map/all_to_all | solution.py:166
  99.1 2.3 %ladder_terms.1 = f32[512,128]{1,0:T(8,128)} custom-call(s32[1,128]{1,0:T(1,128)S(1)} %bitcast.37, f32[2048,128]{1,0:T(8,128)S(1)} %bitcast.31, f32[8,4,16,128]{3,2,1,0:T(8,128)S(1)} %pad_maximum_fusion.refs_0_, f32[8,4,16,128]{3,2,1,0:T(8,128)S(1)} %collective-permute-done.5.__.refs_1_, f32[8,4,16,128]{3,2,1,0:T(8,128)S(1)} %collective-permute-done.4._.refs_2_, ...), custom_call_target="tpu_custom_call" | custom-call | tf_op jit(solution)/shard_map/ladder_terms/pallas_call | solution.py:170
  101.4 3.9 %all-to-all-start.2 = ((f32[32,16,128]{2,1,0:T(8,128)}), f32[32,16,128]{2,1,0:T(8,128)S(1)}, u32[]{:S(2)}, u32[]{:S(2)}) async-start(f32[32,16,128]{2,1,0:T(8,128)} %bitcast.12), calls=%async_computation.2 | async-start | bytes 524288 | tf_op jit(solution)/shard_map/all_to_all | solution.py:179
  105.3 0.1 slice_bitcast_fusion.1
  105.4 0.1 fusion.13
  105.5 8.9 %all-to-all-done.2 = f32[32,16,128]{2,1,0:T(8,128)S(1)} async-done(((f32[32,16,128]{2,1,0:T(8,128)}), f32[32,16,128]{2,1,0:T(8,128)S(1)}, u32[]{:S(2)}, u32[]{:S(2)}) %all-to-all-start.2) | async-done | bytes 262176 | tf_op jit(solution)/shard_map/all_to_all | solution.py:179
  114.4 1.4 gather_fusion
  115.8 23.3 %all-to-all-start.3 = ((f32[128,4,128]{2,1,0:T(4,128)}), f32[128,4,128]{2,1,0:T(4,128)S(1)}, u32[]{:S(2)}, u32[]{:S(2)}) async-start(f32[128,4,128]{2,1,0:T(4,128)} %gather_fusion), calls=%async_computation.3 | async-start | bytes 524288 | tf_op jit(solution)/shard_map/all_to_all | solution.py:116
  139.1 0.0 copy-start.2
  141.7 0.0 copy-start.3
  141.8 0.0 copy-start.4
  141.8 25.5 %all-to-all-done.3 = f32[128,4,128]{2,1,0:T(4,128)S(1)} async-done(((f32[128,4,128]{2,1,0:T(4,128)}), f32[128,4,128]{2,1,0:T(4,128)S(1)}, u32[]{:S(2)}, u32[]{:S(2)}) %all-to-all-start.3) | async-done | bytes 262176 | tf_op jit(solution)/shard_map/all_to_all | solution.py:116
  167.3 0.0 copy-done.2
  167.3 0.0 copy-done.3
  167.3 0.0 copy-done.4
  167.3 0.7 fusion.9
  (5 shorter events, 0.1 us)
Async XLA Ops:
  1.5 33.4 %copy-start = (f32[1,32,16,128]{3,2,1,0:T(8,128)S(1)}, f32[1,32,16,128]{3,2,1,0:T(8,128)}, u32[]{:S(2)}) copy-start(f32[1,32,16,128]{3,2,1,0:T(8,128)} %param.7) | copy-start | bytes 786436
  1.5 70.6 %all-to-all-start = ((f32[128,4,128]{2,1,0:T(4,128)}), f32[128,4,128]{2,1,0:T(4,128)S(1)}, u32[]{:S(2)}, u32[]{:S(2)}) async-start(f32[128,4,128]{2,1,0:T(4,128)} %bitcast.39), calls=%async_computation | async-start | bytes 524288 | tf_op jit(solution)/shard_map/all_to_all | solution.py:116
  34.9 0.7 copy-start.1
  35.7 4.1 %collective-permute-start = (f32[4,4,16,128]{3,2,1,0:T(8,128)S(1)}, f32[4,4,16,128]{3,2,1,0:T(8,128)S(1)}, u32[]{:S(2)}, u32[]{:S(2)}) collective-permute-start(f32[4,4,16,128]{3,2,1,0:T(8,128)S(1)} %get-tuple-element.8), channel_id=1, source_target_pairs={{0,1},{1,0},{2,3},{3,2},{4,5},{5,4},{6,7},{7,6},{8,9},{9,8},{10,11... | collective-permute-start | bytes 393224 | tf_op jit(solution)/shard_map/ppermute | solution.py:150
  39.8 9.0 %collective-permute-start.3 = (f32[2,4,16,128]{3,2,1,0:T(8,128)S(1)}, f32[2,4,16,128]{3,2,1,0:T(8,128)S(1)}, u32[]{:S(2)}, u32[]{:S(2)}) collective-permute-start(f32[2,4,16,128]{3,2,1,0:T(8,128)S(1)} %get-tuple-element.11), channel_id=1, source_target_pairs={{0,6},{2,4},{4,2},{6,0},{1,7},{3,5},{5,3},{7,1},{8,14},{10,12},{12... | collective-permute-start | bytes 196616 | tf_op jit(solution)/shard_map/ppermute | solution.py:152
  44.2 6.8 %collective-permute-start.2 = (f32[2,4,16,128]{3,2,1,0:T(8,128)S(1)}, f32[2,4,16,128]{3,2,1,0:T(8,128)S(1)}, u32[]{:S(2)}, u32[]{:S(2)}) collective-permute-start(f32[2,4,16,128]{3,2,1,0:T(8,128)S(1)} %get-tuple-element.12), channel_id=1, source_target_pairs={{0,4},{2,6},{4,0},{6,2},{1,5},{3,7},{5,1},{7,3},{8,12},{10,14},{12... | collective-permute-start | bytes 196616 | tf_op jit(solution)/shard_map/ppermute | solution.py:152
  46.6 5.3 %collective-permute-start.1 = (f32[2,4,16,128]{3,2,1,0:T(8,128)S(1)}, f32[2,4,16,128]{3,2,1,0:T(8,128)S(1)}, u32[]{:S(2)}, u32[]{:S(2)}) collective-permute-start(f32[2,4,16,128]{3,2,1,0:T(8,128)S(1)} %get-tuple-element.10), channel_id=1, source_target_pairs={{0,2},{2,0},{4,6},{6,4},{1,3},{3,1},{5,7},{7,5},{8,10},{10,8},{12,... | collective-permute-start | bytes 196616 | tf_op jit(solution)/shard_map/ppermute | solution.py:152
  52.0 20.1 %collective-permute-start.4 = (f32[8,4,16,128]{3,2,1,0:T(8,128)S(1)}, f32[8,4,16,128]{3,2,1,0:T(8,128)S(1)}, u32[]{:S(2)}, u32[]{:S(2)}) collective-permute-start(f32[8,4,16,128]{3,2,1,0:T(8,128)S(1)} %pad_maximum_fusion.refs_0_), channel_id=1, source_target_pairs={{0,64},{32,96},{64,0},{96,32},{1,65},{33,97},{65,1},{97,33},{2,66}... | collective-permute-start | bytes 786440 | tf_op jit(solution)/shard_map/ppermute | solution.py:154
  56.0 16.1 %collective-permute-start.5 = (f32[8,4,16,128]{3,2,1,0:T(8,128)S(1)}, f32[8,4,16,128]{3,2,1,0:T(8,128)S(1)}, u32[]{:S(2)}, u32[]{:S(2)}) collective-permute-start(f32[8,4,16,128]{3,2,1,0:T(8,128)S(1)} %pad_maximum_fusion.refs_0_), channel_id=1, source_target_pairs={{0,32},{32,0},{64,96},{96,64},{1,33},{33,1},{65,97},{97,65},{2,34}... | collective-permute-start | bytes 786440 | tf_op jit(solution)/shard_map/ppermute | solution.py:155
  73.5 25.5 %all-to-all-start.1 = ((f32[32,64,128]{2,1,0:T(8,128)}), f32[32,64,128]{2,1,0:T(8,128)S(1)}, u32[]{:S(2)}, u32[]{:S(2)}) async-start(f32[32,64,128]{2,1,0:T(8,128)} %bitcast.10), calls=%async_computation.1 | async-start | bytes 2097152 | tf_op jit(solution)/shard_map/all_to_all | solution.py:166
  82.1 9.6 %collective-permute-start.6 = (f32[8,4,16,128]{3,2,1,0:T(8,128)S(1)}, f32[8,4,16,128]{3,2,1,0:T(8,128)S(1)}, u32[]{:S(2)}, u32[]{:S(2)}) collective-permute-start(f32[8,4,16,128]{3,2,1,0:T(8,128)S(1)} %collective-permute-done.4._.refs_2_), channel_id=1, source_target_pairs={{0,32},{32,0},{64,96},{96,64},{1,33},{33,1},{65,97},{97,65},{2,34}... | collective-permute-start | bytes 786440 | tf_op jit(solution)/shard_map/ppermute | solution.py:156
  101.4 12.9 %all-to-all-start.2 = ((f32[32,16,128]{2,1,0:T(8,128)}), f32[32,16,128]{2,1,0:T(8,128)S(1)}, u32[]{:S(2)}, u32[]{:S(2)}) async-start(f32[32,16,128]{2,1,0:T(8,128)} %bitcast.12), calls=%async_computation.2 | async-start | bytes 524288 | tf_op jit(solution)/shard_map/all_to_all | solution.py:179
  115.8 51.5 %all-to-all-start.3 = ((f32[128,4,128]{2,1,0:T(4,128)}), f32[128,4,128]{2,1,0:T(4,128)S(1)}, u32[]{:S(2)}, u32[]{:S(2)}) async-start(f32[128,4,128]{2,1,0:T(4,128)} %gather_fusion), calls=%async_computation.3 | async-start | bytes 524288 | tf_op jit(solution)/shard_map/all_to_all | solution.py:116
  139.1 28.2 %copy-start.2 = (f32[64,128]{1,0:T(8,128)S(1)}, f32[64,128]{1,0:T(8,128)}, u32[]{:S(2)}) copy-start(f32[64,128]{1,0:T(8,128)} %param.8) | copy-start | bytes 98308
  141.7 25.6 %copy-start.3 = (f32[64]{0:T(128)S(1)}, f32[64]{0:T(128)}, u32[]{:S(2)}) copy-start(f32[64]{0:T(128)} %param.9) | copy-start | bytes 772
  141.8 25.6 %copy-start.4 = (f32[128]{0:T(128)S(1)}, f32[128]{0:T(128)}, u32[]{:S(2)}) copy-start(f32[128]{0:T(128)} %param.10) | copy-start | bytes 1540
